TPU v7x, 32 devices: a whole 2x2x4 slice. The times are simulated.
32 devices in a mesh: dp: 16 (over z, x, core), tensor: 2 (over y).
Axes of the slice: x: 2, y: 2, z: 4, core: 2. Of those that a mesh axis runs over, the one named last changes fastest.
Arguments:
- inputs: bfloat16 [16384, 1024], P(('dp', 'tensor')), may hold values from -6 to 6
- attn_gain: float32 [1024], replicated, may hold values from 0.25 to 1.75
- attn_bias: float32 [1024], replicated, may hold values from -4 to 4
- mlp_gain: float32 [1024], replicated, may hold values from 0.25 to 1.75
- mlp_bias: float32 [1024], replicated, may hold values from -4 to 4
- w_qkv: bfloat16 [1024, 3072], P('dp', 'tensor'), may hold values from -0.1875 to 0.1875
- b_qkv: float32 [3072], P('tensor'), may hold values from -4 to 4
- w_out: bfloat16 [1024, 1024], P('tensor', 'dp'), may hold values from -2 to 2
- b_out: float32 [1024], replicated, may hold values from -4 to 4
- w_up: bfloat16 [1024, 4096], P('dp', 'tensor'), may hold values from -0.1875 to 0.1875
- b_up: float32 [4096], P('tensor'), may hold values from -4 to 4
- w_down: bfloat16 [4096, 1024], P('tensor', 'dp'), may hold values from -0.09375 to 0.09375
- b_down: float32 [1024], replicated, may hold values from -4 to 4
- cotangent: bfloat16 [16384, 1024], P(('dp', 'tensor')), may hold values from -6 to 6
Outputs:
- output: bfloat16 [16384, 1024], P(('dp', 'tensor'))
- grad_inputs: float32 [16384, 1024], P(('dp', 'tensor'))
- grad_attn_gain: float32 [1024], replicated
- grad_attn_bias: float32 [1024], replicated
- grad_mlp_gain: float32 [1024], replicated
- grad_mlp_bias: float32 [1024], replicated
- grad_w_qkv: float32 [1024, 3072], P('dp', 'tensor')
- grad_b_qkv: float32 [3072], P('tensor')
- grad_w_out: float32 [1024, 1024], P('tensor', 'dp')
- grad_b_out: float32 [1024], replicated
- grad_w_up: float32 [1024, 4096], P('dp', 'tensor')
- grad_b_up: float32 [4096], P('tensor')
- grad_w_down: float32 [4096, 1024], P('tensor', 'dp')
- grad_b_down: float32 [1024], replicated
All inputs are finite; a program needn't handle non-finite values.
Results may differ from a plain program's by a relative error of at most 0.012.
Values may be sent and summed in bfloat16 or wider, within the bound.
No kernel may reach another device: no remote copies, remote signals or barrier semaphores. Data moves between devices by JAX's collectives and lax.ppermute only.
A program may use at most 192 MiB of HBM per device.

v0:
```python
import jax
import jax.numpy as jnp
import numpy as np
from jax import lax
from jax.experimental import pallas as pl
from jax.experimental.pallas import tpu as pltpu
from jax.sharding import PartitionSpec as P

HD = 64
ROT = 16
SEQ = 1024
EPSILON = 1e-05
PAIR = 2 * HD
TRIPLE = 6 * HD
BOTH = TRIPLE + PAIR
Q_BLOCK = 256
ROW_BLOCK = 256
UNIT_BLOCK = 512
VMEM_BYTES = 60 * 1024 * 1024
F32 = jnp.float32
BF16 = jnp.bfloat16
ANY = pl.BlockSpec(memory_space=pl.ANY)


def normalize(rows):
    average = jnp.mean(rows, axis=-1, keepdims=True)
    centered = rows - average
    spread = jnp.mean(centered * centered, axis=-1, keepdims=True)
    rate = lax.rsqrt(spread + EPSILON)
    return centered * rate, rate


def rotary_tables(count):
    positions = (np.arange(count) % SEQ).astype(np.float32)
    inverse = (10000.0 ** (-(2.0 * np.arange(ROT // 2)) / ROT)).astype(np.float32)
    angles = (positions[:, None] * inverse[None, :]).astype(np.float64)
    cosine, sine = np.cos(angles), np.sin(angles)
    none = np.zeros_like(sine)
    rest = np.zeros((count, HD - ROT))
    keep = np.concatenate([cosine, cosine, rest + 1.0], axis=1)
    down = np.concatenate([none, sine, rest], axis=1)
    up = np.concatenate([-sine, none, rest], axis=1)
    return tuple(jnp.asarray(np.concatenate([t, t], axis=1), F32) for t in (keep, down, up))


def nn(left, right):
    return jnp.dot(left, right, preferred_element_type=F32)


def nt(left, right):
    return lax.dot_general(left, right, (((1,), (1,)), ((), ())), preferred_element_type=F32)


class Copies:
    def __init__(self, sem):
        self.sem = sem
        self.count = 0
        self.open = []

    def start(self, source, target):
        copy = pltpu.make_async_copy(source, target, self.sem.at[self.count])
        self.count += 1
        copy.start()
        self.open.append(copy)
        return copy

    def rows_in(self, order, parts, columns, target, into):
        copies, at = [], 0
        for part in parts:
            count, rows, _ = part.shape
            for slot in range(count):
                place = pl.ds(pl.multiple_of(order[0, at + slot] * rows, rows), rows)
                copies.append(self.start(part.at[slot, :, columns], target.at[place, into]))
            at += count
        return copies

    def rows_out(self, order, source, outof, parts, columns):
        at = 0
        for part in parts:
            count, rows, _ = part.shape
            for slot in range(count):
                place = pl.ds(pl.multiple_of(order[1, at + slot] * rows, rows), rows)
                self.start(source.at[place, outof], part.at[slot, :, columns])
            at += count

    def wait(self, *copies):
        for copy in copies:
            if copy in self.open:
                self.open.remove(copy)
                copy.wait()

    def wait_all(self):
        self.wait(*list(self.open))


def whole(shape):
    return pl.BlockSpec(shape, lambda i, *_: (0,) * len(shape))


def once(shape):
    return pl.BlockSpec(shape, lambda i, *_: (0,) * len(shape), pipeline_mode=pl.Buffered(1))


def shape_of(shape, dtype):
    return jax.ShapeDtypeStruct(shape, dtype)


def norm_kernel(place, own, other, gains, normed_one, normed_two, one_t, two_t, hat):
    mine = pl.program_id(0) // (pl.num_programs(0) // 2) == place[0]
    rows = jnp.where(mine, own[...], other[...]).astype(F32)
    xhat, _ = normalize(rows)
    one = (xhat * gains[0:1, :] + gains[1:2, :]).astype(BF16)
    two = (xhat * gains[2:3, :] + gains[3:4, :]).astype(BF16)
    normed_one[...] = one
    normed_two[...] = two
    one_t[...] = one.T
    two_t[...] = two.T
    hat[...] = xhat.astype(BF16)


def turn_kernel(place, own, other, rows_out, turned, total):
    mine = pl.program_id(0) // (pl.num_programs(0) // 2) == place[0]
    rows = jnp.where(mine, own[...], other[...])
    rows_out[...] = rows
    turned[...] = rows.T

    @pl.when(pl.program_id(0) == 0)
    def _():
        total[...] = jnp.zeros_like(total)

    @pl.when(mine)
    def _():
        total[...] += jnp.sum(own[...].astype(F32), axis=0, keepdims=True)


def two_sided(kernel, place, own, other, extra, straight, flipped, summed=0):
    rows, width = own.shape
    steps = 2 * rows // ROW_BLOCK
    half = pl.BlockSpec((ROW_BLOCK, width), lambda i, *_: (i % (steps // 2), 0))
    row_spec = pl.BlockSpec((ROW_BLOCK, width), lambda i, *_: (i, 0))
    col_spec = pl.BlockSpec((width, ROW_BLOCK), lambda i, *_: (0, i))
    before, after = straight
    return pl.pallas_call(
        kernel,
        grid_spec=pltpu.PrefetchScalarGridSpec(
            num_scalar_prefetch=1,
            grid=(steps,),
            in_specs=[half, half] + [whole(e.shape) for e in extra],
            out_specs=[row_spec] * before + [col_spec] * flipped + [row_spec] * after + [whole((1, width))] * summed,
        ),
        out_shape=[shape_of((2 * rows, width), BF16)] * before
        + [shape_of((width, 2 * rows), BF16)] * flipped
        + [shape_of((2 * rows, width), BF16)] * after
        + [shape_of((1, width), F32)] * summed,
        compiler_params=pltpu.CompilerParams(vmem_limit_bytes=VMEM_BYTES),
        name=kernel.__name__,
    )(place, own, other, *extra)


def mlp_call(order, n2, n2t, dy, dyt, bias, parts, chunk=(0, 1), buffer=None, init=None, final=None, after=()):
    tokens, width = n2.shape
    _, rows, both = parts[0].shape
    units = both // 2
    block = min(UNIT_BLOCK, units)
    steps = units // block
    n_parts = len(parts)
    slots = sum(part.shape[0] for part in parts)
    chunks = [slice(start, start + ROW_BLOCK) for start in range(0, tokens, ROW_BLOCK)]

    def kernel(order, *refs):
        refs = list(refs)
        take = lambda n: [refs.pop(0) for _ in range(n)]
        take(0 if buffer is None else 1)
        n2_hbm, dy_hbm, n2t_hbm, dyt_hbm, bias = take(5)
        weights = take(n_parts)
        starts = take(2 if init is not None else 0)
        hat_hbm, gain = take(2) if final is not None else (None, None)
        take(len(after))
        grads, gbias, branch_hbm, dnormed_hbm = take(4)
        sums = take(1)[0] if final is not None else None
        n2, dy, n2t, dyt, w, act, dhid, gwide, branch, dnormed, sem = take(11)
        hat = take(1)[0] if final is not None else None
        copies = Copies(sem)
        up = [slice(2 * i * block, (2 * i + 1) * block) for i in range(steps)]
        down = [slice((2 * i + 1) * block, (2 * i + 2) * block) for i in range(steps)]
        unit = [slice(i * block, (i + 1) * block) for i in range(steps)]
        need_up, need_down = [], []
        for i in range(steps):
            need_up.append(copies.rows_in(order, weights, up[i], w, up[i]))
            if i == 0:
                need_up[0].append(copies.start(n2_hbm, n2))
            need_down.append(copies.rows_in(order, weights, down[i], w, down[i]))
            if i == 0:
                need_down[0].append(copies.start(dy_hbm, dy))
        begun = []
        if init is not None:
            begun += [copies.start(starts[0], branch), copies.start(starts[1], dnormed)]
        if final is not None:
            begun += [copies.start(hat_hbm, hat)]
        need_n2t, need_dyt = copies.start(n2t_hbm, n2t), copies.start(dyt_hbm, dyt)
        for i in range(steps):
            total = jnp.zeros((1, block), F32)
            copies.wait(*need_up[i])
            for index, at in enumerate(chunks):
                hidden = nn(n2[at, :], w[:, up[i]]) + bias[:, unit[i]]
                if index == 0:
                    copies.wait(*need_down[i])
                dactive = nn(dy[at, :], w[:, down[i]])
                below = 0.5 + 0.5 * lax.erf(hidden * 0.7071067811865476)
                density = jnp.exp(hidden * hidden * -0.5) * 0.3989422804014327
                dhidden = (dactive * (below + hidden * density)).astype(BF16)
                act[at, unit[i]] = (hidden * below).astype(BF16)
                dhid[at, unit[i]] = dhidden
                total += jnp.sum(dhidden.astype(F32), axis=0, keepdims=True)
            gbias[:, unit[i]] = total
        copies.wait(*begun)
        hat_sum = direct_sum = jnp.zeros((1, width), F32)
        for at in chunks:
            direct = sum(nt(dhid[at, unit[i]], w[:, up[i]]) for i in range(steps))
            mixed = sum(nt(act[at, unit[i]], w[:, down[i]]) for i in range(steps))
            if init is not None:
                direct = direct + dnormed[at, :]
                mixed = mixed + branch[at, :]
            if final is not None:
                hat_sum += jnp.sum(direct * hat[at, :].astype(F32), axis=0, keepdims=True)
                direct_sum += jnp.sum(direct, axis=0, keepdims=True)
                direct = direct * gain[...]
            dnormed[at, :] = direct
            branch[at, :] = mixed
            copies.start(dnormed.at[at, :], dnormed_hbm.at[at, :])
            copies.start(branch.at[at, :], branch_hbm.at[at, :])
        if final is not None:
            sums[0:1, :] = hat_sum
            sums[1:2, :] = direct_sum
        copies.wait(need_n2t, need_dyt)
        for i in range(steps):
            both_at = slice(2 * i * block, (2 * i + 2) * block)
            shifted = slice(chunk[0] * both + 2 * i * block, chunk[0] * both + (2 * i + 2) * block)
            gwide[:, up[i]] = nn(n2t[...], dhid[:, unit[i]]).astype(BF16)
            gwide[:, down[i]] = nn(dyt[...], act[:, unit[i]]).astype(BF16)
            copies.rows_out(order, gwide, both_at, [grads], shifted)
        copies.wait_all()

    square = (tokens, width)
    in_specs = [ANY] * 4 + [whole((1, units))] + [ANY] * n_parts
    operands = [n2, dy, n2t, dyt, bias, *parts]
    out_specs = [ANY, whole((1, units)), ANY, ANY]
    out_shape = [
        shape_of((slots, rows, both * chunk[1]), BF16),
        shape_of((1, units), F32), shape_of(square, F32), shape_of(square, F32),
    ]
    if buffer is not None:
        in_specs = [ANY] + in_specs
        operands = [buffer] + operands
    scratch = [
        pltpu.VMEM(square, BF16), pltpu.VMEM(square, BF16),
        pltpu.VMEM((width, tokens), BF16), pltpu.VMEM((width, tokens), BF16),
        pltpu.VMEM((width, both), BF16), pltpu.VMEM((tokens, units), BF16), pltpu.VMEM((tokens, units), BF16),
        pltpu.VMEM((width, both), BF16), pltpu.VMEM(square, F32), pltpu.VMEM(square, F32),
        pltpu.SemaphoreType.DMA((3 * slots * steps + 2 * len(chunks) + 8,)),
    ]
    if init is not None:
        in_specs += [ANY, ANY]
        operands += list(init)
    if final is not None:
        hat, gain = final
        in_specs += [ANY, whole((1, width))]
        operands += [hat, gain[None]]
        out_specs += [whole((2, width))]
        out_shape += [shape_of((2, width), F32)]
        scratch += [pltpu.VMEM(square, BF16)]
    in_specs += [ANY] * len(after)
    operands += list(after)
    return pl.pallas_call(
        kernel,
        grid_spec=pltpu.PrefetchScalarGridSpec(
            num_scalar_prefetch=1, grid=(1,), in_specs=in_specs, out_specs=out_specs, scratch_shapes=scratch
        ),
        out_shape=out_shape,
        input_output_aliases={} if buffer is None else {1: 0},
        compiler_params=pltpu.CompilerParams(vmem_limit_bytes=VMEM_BYTES),
        cost_estimate=pl.CostEstimate(
            flops=12 * tokens * width * units, transcendentals=2 * tokens * units, bytes_accessed=32 * tokens * width
        ),
        name="mlp_both_ways",
    )(order, *operands)


def attention_call(order, n1, n1t, dy, dyt, tables, bias, parts, outs, call, pairs, init, home_rows, final=None, after=()):
    tokens, width = n1.shape
    rows = parts[0].shape[1]
    n_parts = len(parts)
    slots = sum(part.shape[0] for part in parts) // outs
    half = ROT // 2
    away_rows = tokens - home_rows
    last = final is not None
    shared = away_rows > 0
    share_cuts = [0, away_rows // 4, away_rows]
    wide, narrow = pairs * TRIPLE, pairs * PAIR
    size = wide + narrow
    chunks = [slice(start, start + ROW_BLOCK) for start in range(0, tokens, ROW_BLOCK)]

    def kernel(order, *refs):
        refs = list(refs)
        take = lambda n: [refs.pop(0) for _ in range(n)]
        n1_hbm, dy_hbm, n1t_hbm, dyt_hbm, keep, down, up, bias = take(8)
        weights = take(n_parts)
        starts = take(len(init))
        share_hbm, hat_hbm, gain = take(3) if last else (None, None, None)
        take(len(after))
        grads = take(outs)
        (gbias,) = take(1)
        if last:
            sums, branch_hbm, share_home = take(3)
            outs_away = take(3) if shared else []
        else:
            dnormed_hbm, branch_hbm, outs_away = take(2) + [take(1)]
        n1, dy, n1t, dyt, w, turned, dctx, ctx_t, dq_t, dkv, dmixed, context, gwide, dnormed, branch, sem = take(16)
        away_low = take(1)[0] if shared else None
        share, hat = take(2) if last else (None, None)
        home = pl.multiple_of(order[2, 0] * home_rows, home_rows)
        away = pl.multiple_of(order[2, 1] * away_rows, 16)
        copies = Copies(sem)
        everything = slice(0, size)
        need_w = copies.rows_in(order, weights, slice(call * size, (call + 1) * size), w, everything)
        need_n1 = copies.start(n1_hbm, n1)
        need_dy = copies.start(dy_hbm, dy)
        begun = [copies.start(start, total) for start, total in zip(starts, (branch, dnormed))]
        if last:
            begun += [copies.start(share_hbm, share), copies.start(hat_hbm, hat)]
        need_t = [copies.start(n1t_hbm, n1t), copies.start(dyt_hbm, dyt)]

        def rotate(rows, at, sign):
            lane = lax.broadcasted_iota(jnp.int32, rows[0].shape, 1)
            groups = []
            for index, r in enumerate(rows):
                shift = pltpu.roll(r, half, 1) * down[at, :] + pltpu.roll(r, PAIR - half, 1) * up[at, :]
                turn = r * keep[at, :] + sign * shift
                place = index % 3
                groups.append(turn if place == 0 else jnp.where((lane >= HD) == (place == 1), turn, r))
            return groups

        copies.wait(*need_w, need_n1)
        for at in chunks:
            mixed = nn(n1[at, :], w[:, :wide]) + bias[...]
            for index, group in enumerate(rotate([mixed[:, i * PAIR : (i + 1) * PAIR] for i in range(3 * pairs)], at, 1.0)):
                turned[at, index * PAIR : (index + 1) * PAIR] = group.astype(BF16)
        copies.wait(need_dy)
        dctx[...] = nn(dy[...], w[:, wide:]).astype(BF16)
        behind = lax.broadcasted_iota(jnp.int32, (Q_BLOCK, Q_BLOCK), 0) > lax.broadcasted_iota(
            jnp.int32, (Q_BLOCK, Q_BLOCK), 1
        )
        blank = jnp.zeros((tokens, HD), BF16)
        dkv[...] = jnp.zeros_like(dkv)
        for pair in range(pairs):
            heads = []
            for head in range(2):
                base = pair * TRIPLE + head * 3 * HD
                query = turned[:, base : base + HD] * jnp.asarray(0.125, BF16)
                key = turned[:, base + HD : base + 2 * HD]
                value = turned[:, base + 2 * HD : base + 3 * HD]
                grad = dctx[:, pair * PAIR + head * HD : pair * PAIR + (head + 1) * HD]
                left = jnp.concatenate([query, blank], axis=1)
                right = jnp.concatenate([blank, grad], axis=1)
                heads.append((query, key, value, grad, key.T, value.T, left, right))
            for start in range(0, tokens, Q_BLOCK):
                stop = start + Q_BLOCK
                products = [
                    (nt(key[:stop], query[start:stop]), nt(value[:stop], grad[start:stop]))
                    for query, key, value, grad, *_ in heads
                ]
                mixes = []
                for scores, dprobs in products:
                    edge = jnp.where(behind, -1e30, scores[start:])
                    scores = edge if start == 0 else jnp.concatenate([scores[:start], edge], axis=0)
                    expos = jnp.exp(scores - jnp.max(scores, axis=0, keepdims=True))
                    probs = expos * (1.0 / jnp.sum(expos, axis=0, keepdims=True))
                    inner = jnp.sum(probs * dprobs, axis=0, keepdims=True)
                    mixes.append((probs.astype(BF16), (probs * (dprobs - inner)).astype(BF16)))
                for head, (low, dscores) in enumerate(mixes):
                    _, _, _, _, key_t, value_t, left, right = heads[head]
                    lines = slice(pair * PAIR + head * HD, pair * PAIR + (head + 1) * HD)
                    ctx_t[lines, start:stop] = nn(value_t[:, :stop], low)
                    dq_t[lines, start:stop] = nn(key_t[:, :stop], dscores) * 0.125
                    dkv[2 * pair + head, :stop, :] += nn(dscores, left[start:stop]) + nn(low, right[start:stop])
        context[...] = ctx_t[...].T.astype(BF16)
        if shared and last:
            copies.start(context.at[pl.ds(away, away_rows), :], outs_away[2])
        copies.wait(*begun)
        total = jnp.zeros((1, wide), F32)
        hat_sum = direct_sum = jnp.zeros((1, width), F32)
        for at in chunks:
            rows_before = []
            lane = lax.broadcasted_iota(jnp.int32, (ROW_BLOCK, PAIR), 1)
            for pair in range(pairs):
                dq = dq_t[pair * PAIR : (pair + 1) * PAIR, at].T
                swapped = pltpu.roll(dkv[2 * pair, at, :], HD, 1)
                rows_before += [
                    jnp.where(lane < HD, dq, swapped), jnp.where(lane < HD, swapped, dq), dkv[2 * pair + 1, at, :]
                ]
            low = jnp.concatenate(rotate(rows_before, at, -1.0), axis=1).astype(BF16)
            dmixed[at, :] = low
            total += jnp.sum(low.astype(F32), axis=0, keepdims=True)
            direct = nt(low, w[:, :wide])
            if len(init) > 1:
                direct = direct + dnormed[at, :]
            if last:
                hat_sum += jnp.sum(direct * hat[at, :].astype(F32), axis=0, keepdims=True)
                direct_sum += jnp.sum(direct, axis=0, keepdims=True)
                direct = direct * gain[...] + share[at, :]
            dnormed[at, :] = direct
            if not last:
                copies.start(dnormed.at[at, :], dnormed_hbm.at[at, :])
        gbias[...] = total
        if last:
            sums[0:1, :] = hat_sum
            sums[1:2, :] = direct_sum
            copies.start(dnormed.at[pl.ds(home, home_rows), :], share_home)
            if shared:
                away_low[...] = dnormed[pl.ds(away, away_rows), :].astype(BF16)
                for index in range(2):
                    copies.start(away_low.at[share_cuts[index] : share_cuts[index + 1], :], outs_away[index])
            branch[...] += nt(context[pl.ds(home, home_rows), :], w[:, wide:])
            copies.start(branch, branch_hbm)
        else:
            branch[...] += nt(context[...], w[:, wide:])
            copies.start(branch.at[pl.ds(home, home_rows), :], branch_hbm)
            away_low[...] = branch[pl.ds(away, away_rows), :].astype(BF16)
            copies.start(away_low, outs_away[0])
        copies.wait(*need_t)
        gwide[:, wide:] = nn(dyt[...], context[...]).astype(BF16)
        gwide[:, :wide] = nn(n1t[...], dmixed[...]).astype(BF16)
        copies.rows_out(order, gwide, everything, grads, everything)
        copies.wait_all()

    square = (tokens, width)
    table = whole((tokens, PAIR))
    home, away = (home_rows, width), (away_rows, width)
    in_specs = [ANY] * 4 + [table] * 3 + [pl.BlockSpec((1, wide), lambda i, *_: (0, call))] + [ANY] * (n_parts + len(init))
    operands = [n1, dy, n1t, dyt, *tables, bias, *parts, *init]
    out_specs = [ANY] * outs + [whole((1, wide))]
    out_shape = [shape_of((slots, rows, size), BF16)] * outs + [shape_of((1, wide), F32)]
    scratch = [
        pltpu.VMEM(square, BF16), pltpu.VMEM(square, BF16),
        pltpu.VMEM((width, tokens), BF16), pltpu.VMEM((width, tokens), BF16),
        pltpu.VMEM((width, size), BF16), pltpu.VMEM((tokens, wide), BF16), pltpu.VMEM((tokens, narrow), BF16),
        pltpu.VMEM((narrow, tokens), F32), pltpu.VMEM((narrow, tokens), F32),
        pltpu.VMEM((2 * pairs, tokens, PAIR), F32), pltpu.VMEM((tokens, wide), BF16), pltpu.VMEM((tokens, narrow), BF16),
        pltpu.VMEM((width, size), BF16), pltpu.VMEM(square, F32), pltpu.VMEM(home if last else square, F32),
        pltpu.SemaphoreType.DMA((2 * slots * outs + len(chunks) + 16,)),
    ]
    if shared:
        scratch += [pltpu.VMEM(away, BF16)]
    if last:
        share, hat, gain = final
        in_specs += [ANY, ANY, whole((1, width))]
        operands += [share, hat, gain[None]]
        out_specs += [whole((2, width)), ANY, ANY]
        out_shape += [shape_of((2, width), F32), shape_of(home, F32), shape_of(home, F32)]
        if shared:
            out_specs += [ANY] * 3
            out_shape += [shape_of((share_cuts[i + 1] - share_cuts[i], width), BF16) for i in range(2)]
            out_shape += [shape_of((away_rows, narrow), BF16)]
        scratch += [pltpu.VMEM(square, F32), pltpu.VMEM(square, BF16)]
    else:
        out_specs += [ANY] * 3
        out_shape += [shape_of(square, F32), shape_of(home, F32), shape_of(away, BF16)]
    in_specs += [ANY] * len(after)
    operands += list(after)
    return pl.pallas_call(
        kernel,
        grid_spec=pltpu.PrefetchScalarGridSpec(
            num_scalar_prefetch=1, grid=(1,), in_specs=in_specs, out_specs=out_specs, scratch_shapes=scratch
        ),
        out_shape=out_shape,
        compiler_params=pltpu.CompilerParams(vmem_limit_bytes=VMEM_BYTES),
        cost_estimate=pl.CostEstimate(
            flops=pairs * 20 * tokens * width * BOTH, transcendentals=pairs * tokens * tokens,
            bytes_accessed=32 * tokens * width,
        ),
        name="attention_both_ways",
    )(order, *operands)


def swap_dp(array, bits):
    count = lax.axis_size("dp")
    return lax.ppermute(array, "dp", [(i, i ^ bits) for i in range(count)])


def swap_tensor(array):
    return lax.ppermute(array, "tensor", [(0, 1), (1, 0)])


def hold(arrays, *after):
    def kernel(*refs):
        del refs

    return pl.pallas_call(
        kernel,
        in_specs=[ANY] * (len(arrays) + len(after)),
        out_specs=[ANY] * len(arrays),
        out_shape=[shape_of(a.shape, a.dtype) for a in arrays],
        input_output_aliases={i: i for i in range(len(arrays))},
        name="hold",
    )(*arrays, *after)


def join(pieces, *after):
    rows, width = pieces[0].shape
    block = min(width, 1024)
    count = len(pieces)

    def kernel(*refs):
        out = refs[-1]
        for index in range(count):
            out[index] = refs[index][...]

    return pl.pallas_call(
        kernel,
        grid=(width // block,),
        in_specs=[pl.BlockSpec((rows, block), lambda i: (0, i))] * count + [ANY] * len(after),
        out_specs=pl.BlockSpec((count, rows, block), lambda i: (0, 0, i)),
        out_shape=shape_of((count, rows, width), BF16),
        name="join",
    )(*pieces, *after)


def interleave(pairs, chunks):
    rows = pairs[0][0].shape[0]
    layouts = []
    for (one, other, size_one, size_other), count in zip(pairs, chunks):
        steps = one.shape[1] // size_one // count
        layouts.append((size_one, size_other, steps, count))

    def kernel(*refs):
        ins, outs = refs[: 2 * len(pairs)], list(refs[2 * len(pairs) :])
        for index, (size_one, size_other, steps, count) in enumerate(layouts):
            one, other = ins[2 * index : 2 * index + 2]
            size = size_one + size_other
            for chunk in range(count):
                out = outs.pop(0)
                for step in range(steps):
                    at = chunk * steps + step
                    out[:, step * size : step * size + size_one] = one[:, at * size_one : (at + 1) * size_one]
                    out[:, step * size + size_one : (step + 1) * size] = other[:, at * size_other : (at + 1) * size_other]

    return pl.pallas_call(
        kernel,
        out_shape=[
            shape_of((rows, steps * (size_one + size_other)), BF16)
            for size_one, size_other, steps, count in layouts
            for _ in range(count)
        ],
        name="interleave",
    )(*[array for pair in pairs for array in pair[:2]])


def finish_weights(sources, size_one, size_other):
    size = size_one + size_other
    counts = [len(source) for source in sources]
    widths = [source[0].shape[-1] for source in sources]
    arrays = [array.reshape(array.shape[-2:]) for source in sources for array in source]
    rows = arrays[0].shape[0]
    steps = sum(widths) // size

    def kernel(*refs):
        ins, one, other = list(refs[:-2]), refs[-2], refs[-1]
        at = 0
        for count, width in zip(counts, widths):
            total = ins.pop(0)[...].astype(F32)
            for _ in range(count - 1):
                total = total + ins.pop(0)[...].astype(F32)
            for step in range(width // size):
                base = step * size
                one[:, at * size_one : (at + 1) * size_one] = total[:, base : base + size_one]
                other[:, at * size_other : (at + 1) * size_other] = total[:, base + size_one : base + size]
                at += 1

    return pl.pallas_call(
        kernel,
        out_shape=[shape_of((rows, steps * size_one), F32), shape_of((rows, steps * size_other), F32)],
        name="finish_weights",
    )(*arrays)


def finish_output(inputs, branches, biases, context=None, weights=None, column=0):
    rows, width = inputs.shape
    block = min(rows, 256)
    n_branches = len(branches)
    inner = 0 if context is None else context.shape[1]

    def kernel(x, bias, *refs):
        total = x[...].astype(F32) + bias[0:1, :] + bias[1:2, :]
        for ref in refs[:n_branches]:
            total = total + ref[...].astype(F32)
        if inner:
            total = total + nt(refs[n_branches][...], refs[n_branches + 1][...])
        refs[-1][...] = total.astype(BF16)

    spec = pl.BlockSpec((block, width), lambda i: (i, 0))
    in_specs = [spec, pl.BlockSpec((2, width), lambda i: (0, 0))] + [spec] * n_branches
    operands = [inputs, biases, *branches]
    if inner:
        in_specs += [
            pl.BlockSpec((block, inner), lambda i: (i, 0)), pl.BlockSpec((width, inner), lambda i: (0, column // inner))
        ]
        operands += [context, weights]
    return pl.pallas_call(
        kernel,
        grid=(rows // block,),
        in_specs=in_specs,
        out_specs=spec,
        out_shape=shape_of((rows, width), BF16),
        name="finish_output",
    )(*operands)


def finish_input(inputs, cotangent, home, others, *after):
    rows, width = inputs.shape
    block = min([rows, 128] + [other.shape[0] for other in others])
    starts = np.cumsum([0] + [other.shape[0] // block for other in others])
    count = len(others)

    def kernel(x, dy, home, *refs):
        step = pl.program_id(0)
        share = home[...].astype(F32)
        for index in range(count):
            mine = (step >= starts[index]) & (step < starts[index + 1])
            share = share + jnp.where(mine, refs[index][...].astype(F32), 0.0)
        xhat, rate = normalize(x[...].astype(F32))
        lead = jnp.mean(share, axis=-1, keepdims=True)
        along = jnp.mean(share * xhat, axis=-1, keepdims=True)
        refs[-1][...] = dy[...].astype(F32) + rate * (share - lead - xhat * along)

    def part(index):
        low, high = int(starts[index]), int(starts[index + 1])
        return pl.BlockSpec((block, width), lambda i: (jnp.clip(i - low, 0, high - low - 1), 0))

    spec = pl.BlockSpec((block, width), lambda i: (i, 0))
    return pl.pallas_call(
        kernel,
        grid=(rows // block,),
        in_specs=[spec] * 3 + [part(index) for index in range(count)] + [ANY] * len(after),
        out_specs=spec,
        out_shape=shape_of((rows, width), F32),
        name="finish_input",
    )(inputs, cotangent, home, *others, *after)


def flatten_rows(arrays):
    total = sum(a.shape[0] * a.shape[1] for a in arrays)

    def kernel(*refs):
        out, at = refs[-1], 0
        for ref in refs[:-1]:
            count, width = ref.shape
            for row in range(count):
                out[:, at : at + width] = ref[row : row + 1, :]
                at += width

    return pl.pallas_call(kernel, out_shape=shape_of((1, total), F32), name="flatten_rows")(*arrays)


def add_split(pairs, sizes):
    count, rows, width = pairs[0][0].shape
    block = min(width, 512)
    steps = width // block

    def kernel(*refs):
        ins, outs = refs[: 2 * len(pairs)], refs[2 * len(pairs) :]
        for index in range(len(pairs)):
            left, right = ins[2 * index : 2 * index + 2]

            @pl.when(pl.program_id(0) // steps == index)
            def _():
                at = 0
                for size, out in zip(sizes, outs):
                    total = left[at : at + size].astype(F32) + right[at : at + size].astype(F32)
                    out[...] = total.astype(BF16)
                    at += size

    def part(index):
        return pl.BlockSpec((count, rows, block), lambda i: (0, 0, jnp.clip(i - index * steps, 0, steps - 1)))

    return pl.pallas_call(
        kernel,
        grid=(len(pairs) * steps,),
        in_specs=[part(index) for index in range(len(pairs)) for _ in range(2)],
        out_specs=[pl.BlockSpec((size, rows, block), lambda i: (0, 0, i)) for size in sizes],
        out_shape=[shape_of((size, rows, len(pairs) * width), BF16) for size in sizes],
        name="add_split",
    )(*[array for pair in pairs for array in pair])


def relative_order(weights):
    slots = np.arange(16)
    bits = (slots % 4) * 4 + (slots // 4 % 2) * weights[0] + (slots // 8) * weights[1]
    return jnp.asarray(bits, jnp.int32) ^ lax.axis_index("dp").astype(jnp.int32)


def gather_lines(piece, *after):
    return join([piece] + [swap_dp(piece, 4 * s) for s in (1, 2, 3)], *after)


def send_lines(lines):
    return [lines[0]] + [swap_dp(lines[s], 4 * s) for s in (1, 2, 3)]


def on_device(
    inputs, attn_gain, attn_bias, mlp_gain, mlp_bias, w_qkv, b_qkv, w_out, b_out, w_up, b_up, w_down, b_down, cotangent
):
    own_rows, width = inputs.shape
    units = w_up.shape[1]
    columns = w_qkv.shape[1]
    pairs = columns // TRIPLE
    piece_rows = w_up.shape[0]
    n_dp, n_tensor = lax.axis_size("dp"), lax.axis_size("tensor")
    by_hand = n_dp == 16 and n_tensor == 2
    block = min(UNIT_BLOCK, units)
    gains = jnp.stack([attn_gain, attn_bias, mlp_gain, mlp_bias])
    natural = jnp.arange(n_dp, dtype=jnp.int32)
    side = lax.axis_index("tensor").astype(jnp.int32)
    tables = rotary_tables(own_rows * n_tensor)

    def full_gather(piece):
        return lax.all_gather(piece, "dp", axis=0, tiled=True).reshape(n_dp, piece_rows, piece.shape[1])

    def full_scatter(parts):
        return lax.psum_scatter(parts.reshape(width, parts.shape[2]), "dp", scatter_dimension=0, tiled=True)

    biases = jnp.stack([b_out, b_down])
    if by_hand:
        sides = jnp.zeros((n_dp,), jnp.int32).at[0].set(side).at[1].set(1 - side)
        arrive, leave = relative_order((1, 2)), relative_order((2, 1))
        place = side[None]
        piece_a, piece_b, attn_piece = interleave(
            [(w_up, w_down.T, block, block), (w_qkv, w_out.T, pairs // 2 * TRIPLE, pairs // 2 * PAIR)], (2, 1)
        )
        first = pairs // 2
        later = (pairs - first) * PAIR
        x_other = swap_tensor(inputs)
        out_other = swap_tensor(w_out.T[:, first * PAIR :])
        lines_a = gather_lines(piece_a, x_other, out_other)
        held_dy, piece_b = hold([cotangent, piece_b], lines_a)
        dy_other = swap_tensor(held_dy)
        lines_b = gather_lines(piece_b)
        n1, n2, n1t, n2t, hat = two_sided(norm_kernel, place, inputs, x_other, [gains], (2, 1), 2)
        attn_piece = jnp.concatenate([attn_piece, out_other], axis=1)
        across_a, lines_b, attn_piece = hold([swap_dp(lines_a, 2), lines_b, attn_piece], n1, dy_other)
        attn_wide = full_gather(attn_piece)
        attn_parts = [attn_wide]
        parts_a = [lines_a, swap_dp(lines_a, 1), across_a, swap_dp(across_a, 1)]
        dy, dyt, dy_sum = two_sided(turn_kernel, place, cotangent, dy_other, [], (1, 0), 1, 1)

        order = jnp.stack([arrive, natural])
        buffer, gb_a, branch, dn2 = mlp_call(
            order, n2, n2t, dy, dyt, b_up[None, : units // 2], parts_a, chunk=(0, 2), after=[lines_b]
        )
        (across_b,) = hold([swap_dp(lines_b, 2)], gb_a)
        parts_b = [lines_b, swap_dp(lines_b, 1), across_b, swap_dp(across_b, 1)]
        wide, gb_b, branch, share, sums_two = mlp_call(
            order, n2, n2t, dy, dyt, b_up[None, units // 2 :], parts_b, chunk=(1, 2), buffer=buffer,
            init=(branch, dn2), final=(hat, mlp_gain),
        )
        mlp_sum = full_scatter(wide)
        attn_order = jnp.stack([natural, leave, sides])
        keep_c, send_c, gb_c, dn1, branch_home, branch_away = attention_call(
            attn_order, n1, n1t, dy, dyt, tables, b_qkv[None], attn_parts, 2, 0, first, (branch,), own_rows
        )
        branch_other = swap_tensor(branch_away)
        low_c, high_c = add_split([(keep_c, swap_dp(send_c, 1))], (4, 4))
        keep_d, send_d, gb_d, sums_one, branch_home, share_home, *share_away, ctx_away = attention_call(
            attn_order, n1, n1t, dy, dyt, tables, b_qkv[None], attn_parts, 2, 1, pairs - first,
            (branch_home, dn1), own_rows, final=(share, hat, attn_gain), after=[high_c],
        )
        across_c, branch_other, ctx_away, send_d, gb_d, *share_away = hold(
            [swap_dp(high_c, 2), branch_other, ctx_away, send_d, gb_d, *share_away]
        )
        small = flatten_rows([gb_c, gb_d, gb_a, gb_b, sums_one, sums_two, dy_sum])
        across_d, keep_d, small_other = hold([swap_dp(send_d, 1), keep_d, swap_dp(small, 1)])
        low_d, high_d = add_split([(keep_d, across_d)], (4, 4))
        small = small + small_other
        share_first, ctx_away = hold([share_away[0], ctx_away], high_d)
        across_d, share_first, ctx_other, *small_others = hold(
            [
                swap_dp(high_d, 2), swap_tensor(share_first), swap_tensor(ctx_away),
                swap_dp(small, 4), swap_dp(small, 8), swap_dp(small, 12),
            ]
        )
        small = sum(small_others, small)
        lines = add_split([(low_c, across_c), (low_d, across_d)], (1, 1, 1, 1))
        sent = send_lines(lines)
        share_second, small = hold([share_away[1], small], *lines)
        output = finish_output(
            inputs, [branch_home, branch_other], biases, ctx_other, attn_wide.reshape(width, -1), columns + pairs * PAIR
        )
        share_second, small_other, *sent = hold(
            [swap_tensor(share_second), swap_dp(small, 2), *sent], output
        )
        small = small + small_other
        small = small + swap_tensor(jnp.where(jnp.arange(small.shape[1]) < columns + units, 0.0, small))
        grad_inputs = finish_input(inputs, cotangent, share_home, [share_first, share_second])
        (mlp_sum,) = hold([mlp_sum], grad_inputs)
        grad_up, grad_down_t = finish_weights([[mlp_sum]], block, block)
        attn_sources = [sent]
        small = small[0]
        tail = small[columns + units :]
    else:
        mlp_piece, attn_piece = interleave(
            [(w_up, w_down.T, block, block), (w_qkv, w_out.T, columns, pairs * PAIR)], (1, 1)
        )
        order = jnp.stack([natural, natural, jnp.zeros_like(natural)])
        x = lax.all_gather(inputs, "tensor", axis=0, tiled=True)
        dy = lax.all_gather(cotangent, "tensor", axis=0, tiled=True)
        mlp_parts = [full_gather(mlp_piece)]
        attn_parts = [full_gather(attn_piece)]
        rows = x.shape[0]
        place = jnp.zeros((1,), jnp.int32)
        n1, n2, n1t, n2t, hat = two_sided(
            norm_kernel, place, x[: rows // 2], x[rows // 2 :], [gains], (2, 1), 2
        )
        dy, dyt, _ = two_sided(turn_kernel, place, dy[: rows // 2], dy[rows // 2 :], [], (1, 0), 1, 1)
        wide, gb_up, branch, share, sums_two = mlp_call(
            order[:2], n2, n2t, dy, dyt, b_up[None], mlp_parts, final=(hat, mlp_gain)
        )
        narrow, gb_qkv, sums_one, branch, share = attention_call(
            order, n1, n1t, dy, dyt, tables, b_qkv[None], attn_parts, 1, 0, pairs, (branch,), rows,
            final=(share, hat, attn_gain),
        )
        grad_up, grad_down_t = finish_weights([[full_scatter(wide)]], block, block)
        attn_sources = [[full_scatter(narrow)]]
        share = lax.psum_scatter(share.astype(BF16), "tensor", scatter_dimension=0, tiled=True)
        branch = lax.psum_scatter(branch.astype(BF16), "tensor", scatter_dimension=0, tiled=True)
        output = finish_output(inputs, [branch], biases)
        grad_inputs = finish_input(inputs, cotangent, share, [])
        small = lax.psum(jnp.concatenate([gb_qkv[0], gb_up[0]]), "dp")
        own_sum = jnp.sum(cotangent.astype(F32), axis=0)
        tail = lax.psum(jnp.concatenate([sums_one.reshape(-1), sums_two.reshape(-1), own_sum]), ("dp", "tensor"))

    sums = tail.reshape(5, width)
    calls = 2 if by_hand else 1
    grad_qkv, grad_out_t = finish_weights(attn_sources, columns // calls, pairs // calls * PAIR)
    return (
        output,
        grad_inputs,
        sums[0],
        sums[1],
        sums[2],
        sums[3],
        grad_qkv,
        small[:columns],
        grad_out_t.T,
        sums[4],
        grad_up,
        small[columns : columns + units],
        grad_down_t.T,
        sums[4],
    )


def solution(mesh):
    rows = P(("dp", "tensor"), None)
    return jax.shard_map(
        on_device,
        mesh=mesh,
        in_specs=(
            rows, P(), P(), P(), P(), P("dp", "tensor"), P("tensor"), P("tensor", "dp"), P(),
            P("dp", "tensor"), P("tensor"), P("tensor", "dp"), P(), rows,
        ),
        out_specs=(
            rows, rows, P(), P(), P(), P(), P("dp", "tensor"), P("tensor"), P("tensor", "dp"), P(),
            P("dp", "tensor"), P("tensor"), P("tensor", "dp"), P(),
        ),
        check_vma=False,
    )
```

profile of v0, /device:TPU:8, one launch (start us, length us, event | category | flops | bytes accessed | tf_op | source)
XLA Modules:
  0.0 286.9 jit_solution(11751928021399421586)
XLA Ops:
  7.2 1.6 collective-permute-start
  8.8 2.0 interleave.1
  11.2 2.6 collective-permute-start.2
  15.5 2.3 copy.68.refs_0_
  17.9 15.3 %collective-permute-done.4.refs_5_ = bf16[64,256]{1,0:T(8,128)(2,1)S(1)} collective-permute-done((bf16[64,256]{1,0:T(8,128)(2,1)S(1)}, bf16[64,256]{1,0:T(8,128)(2,1)S(1)}, u32[]{:S(2)}, u32[]{:S(2)}) %collective-permute-start.4) | collective-permute-done | bytes 32800 | tf_op jit(solution)/shard_map/ppermute | solution.py:491
  33.1 3.7 %collective-permute-done.3.refs_3_ = bf16[64,2048]{1,0:T(8,128)(2,1)S(1)} collective-permute-done((bf16[64,2048]{1,0:T(8,128)(2,1)}, bf16[64,2048]{1,0:T(8,128)(2,1)S(1)}, u32[]{:S(2)}, u32[]{:S(2)}) %collective-permute-start.3) | collective-permute-done | bytes 262176 | tf_op jit(solution)/shard_map/ppermute | solution.py:487
  37.6 1.0 copy-done
  38.5 2.1 join.2.refs_2_.refs_5_
  41.9 1.5 collective-permute-start.6
  44.0 3.0 %collective-permute-start.8 = (bf16[64,2048]{1,0:T(8,128)(2,1)}, bf16[64,2048]{1,0:T(8,128)(2,1)}, u32[]{:S(2)}, u32[]{:S(2)}) collective-permute-start(bf16[64,2048]{1,0:T(8,128)(2,1)} %get-tuple-element.123.refs_0_), channel_id=1, source_target_pairs={{0,16},{2,18},{4,20},{6,22},{8,24},{10,26},{12,28},{14,30},{16,0},... | collective-permute-start | bytes 786440 | tf_op jit(solution)/shard_map/ppermute | solution.py:487
  48.2 7.3 %norm_kernel.1 = (bf16[1024,1024]{1,0:T(8,128)(2,1)}, bf16[1024,1024]{1,0:T(8,128)(2,1)}, bf16[1024,1024]{1,0:T(8,128)(2,1)}, bf16[1024,1024]{1,0:T(8,128)(2,1)}, bf16[1024,1024]{1,0:T(8,128)(2,1)}) custom-call(s32[1]{0:T(128)} %bitcast.3.place, bf16[512,1024]{1,0:T(8,128)(2,1)} %x.5, bf16[512,1024]{1,0:T(8,128)(2,1)} %copy-done, ...), custom_call_target="tpu_custom_call" | custom-call | tf_op jit(solution)/shard_map/norm_kernel/pallas_call | solution.py:143
  55.5 9.0 %collective-permute-done.8.refs_2_ = bf16[64,2048]{1,0:T(8,128)(2,1)} collective-permute-done((bf16[64,2048]{1,0:T(8,128)(2,1)}, bf16[64,2048]{1,0:T(8,128)(2,1)}, u32[]{:S(2)}, u32[]{:S(2)}) %collective-permute-start.8) | collective-permute-done | bytes 262176 | tf_op jit(solution)/shard_map/ppermute | solution.py:487
  64.5 4.2 %collective-permute-done.9.refs_3_ = bf16[64,2048]{1,0:T(8,128)(2,1)} collective-permute-done((bf16[64,2048]{1,0:T(8,128)(2,1)}, bf16[64,2048]{1,0:T(8,128)(2,1)}, u32[]{:S(2)}, u32[]{:S(2)}) %collective-permute-start.9) | collective-permute-done | bytes 262176 | tf_op jit(solution)/shard_map/ppermute | solution.py:487
  68.8 2.2 join.3.refs_1_
  70.9 0.9 copy-done.4
  74.7 5.4 %turn_kernel.1 = (bf16[1024,1024]{1,0:T(8,128)(2,1)}, bf16[1024,1024]{1,0:T(8,128)(2,1)}, f32[1,1024]{1,0:T(1,128)}) custom-call(s32[1]{0:T(128)} %bitcast.3.place, bf16[512,1024]{1,0:T(8,128)(2,1)} %dy.1, bf16[512,1024]{1,0:T(8,128)(2,1)} %copy-done.4), custom_call_target="tpu_custom_call" | custom-call | tf_op jit(solution)/shard_map/turn_kernel/pallas_call | solution.py:143
  80.1 21.6 %mlp_both_ways.2 = (bf16[16,64,4096]{2,1,0:T(8,128)(2,1)}, f32[1,1024]{1,0:T(1,128)}, f32[1024,1024]{1,0:T(8,128)}, f32[1024,1024]{1,0:T(8,128)}) custom-call(s32[2,16]{1,0:T(2,128)} %pad_add_fusion.1.order, bf16[1024,1024]{1,0:T(8,128)(2,1)} %get-tuple-element.126.refs_0_.refs_1_, bf16[1024,1024]{1,0:T(8,128)(2,1)} %get-tuple-element.120.refs_1_.refs_2_, ...), custom_call_target="tpu_custom_call" | custom-call | flops 12884901888 | bytes 33554432 | tf_op jit(solution)/shard_map/mlp_both_ways/pallas_call | solution.py:274
  101.7 1.0 collective-permute-done.13.refs_0_
  102.6 1.0 copy-done.8
  103.6 2.9 collective-permute-done.14.refs_9_
  106.5 1.0 copy-done.43
  107.5 22.8 %mlp_both_ways.3 = (bf16[16,64,4096]{2,1,0:T(8,128)(2,1)}, f32[1,1024]{1,0:T(1,128)}, f32[1024,1024]{1,0:T(8,128)}, f32[1024,1024]{1,0:T(8,128)}, f32[2,1024]{1,0:T(2,128)}) custom-call(s32[2,16]{1,0:T(2,128)} %pad_add_fusion.1.order, bf16[16,64,4096]{2,1,0:T(8,128)(2,1)} %get-tuple-element.130.refs_0_, ...), custom_call_target="tpu_custom_call", output_to_operand_aliasing={{0}: (1, {})} | custom-call | flops 12884901888 | bytes 33554432 | tf_op jit(solution)/shard_map/mlp_both_ways/pallas_call | solution.py:274
  132.2 27.0 %attention_both_ways.2 = (bf16[8,64,1024]{2,1,0:T(8,128)(2,1)}, bf16[8,64,1024]{2,1,0:T(8,128)(2,1)}, f32[1,768]{1,0:T(1,128)}, f32[1024,1024]{1,0:T(8,128)}, f3...) custom-call(s32[3,16]{1,0:T(4,128)} %pad_add_fusion.order, bf16[1024,1024]{1,0:T(8,128)(2,1)} %get-tuple-element.116.refs_3_.refs_0_, ...), custom_call_target="tpu_custom_call" | custom-call | flops 21474836480 | bytes 33554432 | tf_op jit(solution)/shard_map/attention_both_ways/pallas_call | solution.py:470
  160.1 2.1 collective-permute-done.15.refs_1_
  162.2 1.0 copy-done.9
  163.2 2.4 add_split.3
  166.3 26.8 %attention_both_ways.3 = (bf16[8,64,1024]{2,1,0:T(8,128)(2,1)}, bf16[8,64,1024]{2,1,0:T(8,128)(2,1)}, f32[1,768]{1,0:T(1,128)}, f32[2,1024]{1,0:T(2,128)}, f32[5...) custom-call(s32[3,16]{1,0:T(4,128)} %pad_add_fusion.order, ...), custom_call_target="tpu_custom_call" | custom-call | flops 21474836480 | bytes 33554432 | tf_op jit(solution)/shard_map/attention_both_ways/pallas_call | solution.py:470
  194.3 1.4 flatten_rows.1
  196.2 1.1 collective-permute-done.19.refs_2_
  198.3 2.5 add_split.4
  200.8 1.3 collective-permute-start.20
  202.6 1.5 collective-permute-start.22
  204.2 3.0 %collective-permute-start.24 = (f32[1,8704]{1,0:T(1,128)S(1)}, f32[1,8704]{1,0:T(1,128)S(1)}, u32[]{:S(2)}, u32[]{:S(2)}) collective-permute-start(f32[1,8704]{1,0:T(1,128)S(1)} %add.26), channel_id=1, source_target_pairs={{0,16},{2,18},{4,20},{6,22},{8,24},{10,26},{12,28},{14,30},{16,0},... | collective-permute-start | bytes 104456 | tf_op jit(solution)/shard_map/ppermute | solution.py:487
  208.2 1.5 collective-permute-start.25
  209.7 2.4 collective-permute-done.25.refs_5_
  212.1 4.1 %collective-permute-done.22.refs_2_ = bf16[512,256]{1,0:T(8,128)(2,1)S(1)} collective-permute-done((bf16[512,256]{1,0:T(8,128)(2,1)}, bf16[512,256]{1,0:T(8,128)(2,1)S(1)}, u32[]{:S(2)}, u32[]{:S(2)}) %collective-permute-start.22) | collective-permute-done | bytes 262176 | tf_op jit(solution)/shard_map/ppermute | solution.py:491
  217.7 4.0 %add_split.5 = (bf16[1,64,2048]{2,1,0:T(8,128)(2,1)}, bf16[1,64,2048]{2,1,0:T(8,128)(2,1)}, bf16[1,64,2048]{2,1,0:T(8,128)(2,1)}, bf16[1,64,2048]{2,1,0:T(8,128)(2,1)}) custom-call(bf16[4,64,1024]{2,1,0:T(8,128)(2,1)} %get-tuple-element.173.refs_0_, bf16[4,64,1024]{2,1,0:T(8,128)(2,1)} %get-tuple-element.174.refs_1_, ...), custom_call_target="tpu_custom_call" | custom-call | tf_op jit(solution)/shard_map/add_split/pallas_call | solution.py:685
  222.4 1.0 collective-permute-start.26
  223.8 3.1 %collective-permute-start.29 = (bf16[1,64,2048]{2,1,0:T(8,128)(2,1)}, bf16[1,64,2048]{2,1,0:T(8,128)(2,1)S(1)}, u32[]{:S(2)}, u32[]{:S(2)}) collective-permute-start(bf16[1,64,2048]{2,1,0:T(8,128)(2,1)} %get-tuple-element.179.refs_4_), channel_id=1, source_target_pairs={{0,16},{2,18},{4,20},{6,22},{8,24},{10,26},{12,28},{14,30},{16,0},... | collective-permute-start | bytes 786440 | tf_op jit(solution)/shard_map/ppermute | solution.py:487
  226.9 2.2 collective-permute-start.27
  229.8 3.6 %finish_output.1.refs_6_ = bf16[512,1024]{1,0:T(8,128)(2,1)} custom-call(bf16[512,1024]{1,0:T(8,128)(2,1)} %x.5, f32[2,1024]{1,0:T(2,128)} %pad_maximum_fusion.2.bias, f32[512,1024]{1,0:T(8,128)} %get-tuple-element.142.refs_0_, bf16[512,1024]{1,0:T(8,128)(2,1)} %get-tuple-element.149.refs_1_, bf16[512,256]{1,0:T(8,128)(2,1)} %get-tuple-element.166.refs_2_, ...), custom_call_target="tpu_custom_call" | custom-call | tf_op jit(solution)/shard_map/finish_output/pallas_call | solution.py:608
  233.4 13.3 %collective-permute-done.28.refs_3_ = bf16[1,64,2048]{2,1,0:T(8,128)(2,1)S(1)} collective-permute-done((bf16[1,64,2048]{2,1,0:T(8,128)(2,1)}, bf16[1,64,2048]{2,1,0:T(8,128)(2,1)S(1)}, u32[]{:S(2)}, u32[]{:S(2)}) %collective-permute-start.28) | collective-permute-done | bytes 262176 | tf_op jit(solution)/shard_map/ppermute | solution.py:487
  246.7 4.4 %collective-permute-done.29.refs_4_ = bf16[1,64,2048]{2,1,0:T(8,128)(2,1)S(1)} collective-permute-done((bf16[1,64,2048]{2,1,0:T(8,128)(2,1)}, bf16[1,64,2048]{2,1,0:T(8,128)(2,1)S(1)}, u32[]{:S(2)}, u32[]{:S(2)}) %collective-permute-start.29) | collective-permute-done | bytes 262176 | tf_op jit(solution)/shard_map/ppermute | solution.py:487
  251.1 12.9 %collective-permute-done.30.refs_5_ = bf16[1,64,2048]{2,1,0:T(8,128)(2,1)S(1)} collective-permute-done((bf16[1,64,2048]{2,1,0:T(8,128)(2,1)}, bf16[1,64,2048]{2,1,0:T(8,128)(2,1)S(1)}, u32[]{:S(2)}, u32[]{:S(2)}) %collective-permute-start.30) | collective-permute-done | bytes 262176 | tf_op jit(solution)/shard_map/ppermute | solution.py:487
  266.4 1.5 collective-permute-start.31
  268.0 5.2 %finish_input.1.refs_1_ = f32[512,1024]{1,0:T(8,128)} custom-call(bf16[512,1024]{1,0:T(8,128)(2,1)} %x.5, bf16[512,1024]{1,0:T(8,128)(2,1)} %dy.1, f32[512,1024]{1,0:T(8,128)} %get-tuple-element.167.home, bf16[128,1024]{1,0:T(8,128)(2,1)} %get-tuple-element.168.refs_0_, bf16[384,1024]{1,0:T(8,128)(2,1)} %get-tuple-element.183.refs_1_), custom_call_target="tpu_custom_call" | custom-call | tf_op jit(solution)/shard_map/finish_input/pallas_call | solution.py:640
  273.2 2.1 finish_weights.2
  277.2 2.1 finish_weights.3
  (164 shorter events, 24.6 us)
Async XLA Ops:
  7.2 125.1 %all-gather.2.cloned.1.call-start = ((), (), s32[]{:S(2)}) async-start(), calls=%async_computation.1 | async-start | bytes 5013504 | tf_op jit(solution)/shard_map/all_gather | solution.py:726
  7.2 29.6 %collective-permute-start = (bf16[512,1024]{1,0:T(8,128)(2,1)}, bf16[512,1024]{1,0:T(8,128)(2,1)S(1)}, u32[]{:S(2)}, u32[]{:S(2)}) collective-permute-start(bf16[512,1024]{1,0:T(8,128)(2,1)} %x.5), channel_id=1, source_target_pairs={{0,1},{1,0},{2,3},{3,2},{4,5},{5,4},{6,7},{7,6},{8,9},{9,8},{10,11... | collective-permute-start | bytes 3145736 | tf_op jit(solution)/shard_map/ppermute | solution.py:491
  10.8 22.3 %collective-permute-start.1 = (bf16[64,2048]{1,0:T(8,128)(2,1)}, bf16[64,2048]{1,0:T(8,128)(2,1)S(1)}, u32[]{:S(2)}, u32[]{:S(2)}) collective-permute-start(bf16[64,2048]{1,0:T(8,128)(2,1)} %get-tuple-element.118.refs_0_), channel_id=1, source_target_pairs={{0,8},{2,10},{4,12},{6,14},{8,0},{10,2},{12,4},{14,6},{16,24},{18,... | collective-permute-start | bytes 786440 | tf_op jit(solution)/shard_map/ppermute | solution.py:487
  11.2 21.9 %collective-permute-start.2 = (bf16[64,2048]{1,0:T(8,128)(2,1)}, bf16[64,2048]{1,0:T(8,128)(2,1)S(1)}, u32[]{:S(2)}, u32[]{:S(2)}) collective-permute-start(bf16[64,2048]{1,0:T(8,128)(2,1)} %get-tuple-element.118.refs_0_), channel_id=1, source_target_pairs={{0,16},{2,18},{4,20},{6,22},{8,24},{10,26},{12,28},{14,30},{16,0},... | collective-permute-start | bytes 786440 | tf_op jit(solution)/shard_map/ppermute | solution.py:487
  13.8 23.0 %collective-permute-start.3 = (bf16[64,2048]{1,0:T(8,128)(2,1)}, bf16[64,2048]{1,0:T(8,128)(2,1)S(1)}, u32[]{:S(2)}, u32[]{:S(2)}) collective-permute-start(bf16[64,2048]{1,0:T(8,128)(2,1)} %get-tuple-element.118.refs_0_), channel_id=1, source_target_pairs={{0,24},{2,26},{4,28},{6,30},{8,16},{10,18},{12,20},{14,22},{16,8},... | collective-permute-start | bytes 786440 | tf_op jit(solution)/shard_map/ppermute | solution.py:487
  15.0 18.1 %collective-permute-start.4 = (bf16[64,256]{1,0:T(8,128)(2,1)S(1)}, bf16[64,256]{1,0:T(8,128)(2,1)S(1)}, u32[]{:S(2)}, u32[]{:S(2)}) collective-permute-start(bf16[64,256]{1,0:T(8,128)(2,1)S(1)} %slice.80), channel_id=1, source_target_pairs={{0,1},{1,0},{2,3},{3,2},{4,5},{5,4},{6,7},{7,6},{8,9},{9,8},{10,11... | collective-permute-start | bytes 98312 | tf_op jit(solution)/shard_map/ppermute | solution.py:491
  17.8 25.6 %copy-start.38 = (f32[1024]{0:T(1024)S(1)}, f32[1024]{0:T(1024)}, u32[]{:S(2)}) copy-start(f32[1024]{0:T(1024)} %param.27) | copy-start | bytes 12292
  17.8 25.6 %copy-start.39 = (f32[1024]{0:T(1024)S(1)}, f32[1024]{0:T(1024)}, u32[]{:S(2)}) copy-start(f32[1024]{0:T(1024)} %param.25) | copy-start | bytes 12292
  17.8 25.6 %copy-start.40 = (f32[1024]{0:T(1024)S(1)}, f32[1024]{0:T(1024)}, u32[]{:S(2)}) copy-start(f32[1024]{0:T(1024)} %param.26) | copy-start | bytes 12292
  17.8 25.6 %copy-start.41 = (f32[1024]{0:T(1024)S(1)}, f32[1024]{0:T(1024)}, u32[]{:S(2)}) copy-start(f32[1024]{0:T(1024)} %param.24) | copy-start | bytes 12292
  17.8 29.7 %copy-start.20 = (bf16[64,2048]{1,0:T(8,128)(2,1)S(1)}, bf16[64,2048]{1,0:T(8,128)(2,1)}, u32[]{:S(2)}) copy-start(bf16[64,2048]{1,0:T(8,128)(2,1)} %get-tuple-element.124) | copy-start | bytes 786436
  40.7 6.8 %copy-start.32 = (bf16[64,256]{1,0:T(8,128)(2,1)S(1)}, bf16[64,256]{1,0:T(8,128)(2,1)}, u32[]{:S(2)}) copy-start(bf16[64,256]{1,0:T(8,128)(2,1)} %copy-done.31) | copy-start | bytes 98308
  40.7 30.2 %collective-permute-start.5 = (bf16[512,1024]{1,0:T(8,128)(2,1)}, bf16[512,1024]{1,0:T(8,128)(2,1)S(1)}, u32[]{:S(2)}, u32[]{:S(2)}) collective-permute-start(bf16[512,1024]{1,0:T(8,128)(2,1)} %get-tuple-element.119), channel_id=1, source_target_pairs={{0,1},{1,0},{2,3},{3,2},{4,5},{5,4},{6,7},{7,6},{8,9},{9,8},{10,11... | collective-permute-start | bytes 3145736 | tf_op jit(solution)/shard_map/ppermute | solution.py:491
  41.9 29.0 %collective-permute-start.6 = (bf16[4,64,2048]{2,1,0:T(8,128)(2,1)S(1)}, bf16[4,64,2048]{2,1,0:T(8,128)(2,1)S(1)}, u32[]{:S(2)}, u32[]{:S(2)}) collective-permute-start(bf16[4,64,2048]{2,1,0:T(8,128)(2,1)S(1)} %copy-done.1), channel_id=1, source_target_pairs={{0,4},{2,6},{4,0},{6,2},{8,12},{10,14},{12,8},{14,10},{16,20},{18,... | collective-permute-start | bytes 3145736 | tf_op jit(solution)/shard_map/ppermute | solution.py:487
  44.0 11.5 %collective-permute-start.7 = (bf16[64,2048]{1,0:T(8,128)(2,1)}, bf16[64,2048]{1,0:T(8,128)(2,1)}, u32[]{:S(2)}, u32[]{:S(2)}) collective-permute-start(bf16[64,2048]{1,0:T(8,128)(2,1)} %get-tuple-element.123.refs_0_), channel_id=1, source_target_pairs={{0,8},{2,10},{4,12},{6,14},{8,0},{10,2},{12,4},{14,6},{16,24},{18,... | collective-permute-start | bytes 786440 | tf_op jit(solution)/shard_map/ppermute | solution.py:487
  44.0 20.5 %collective-permute-start.8 = (bf16[64,2048]{1,0:T(8,128)(2,1)}, bf16[64,2048]{1,0:T(8,128)(2,1)}, u32[]{:S(2)}, u32[]{:S(2)}) collective-permute-start(bf16[64,2048]{1,0:T(8,128)(2,1)} %get-tuple-element.123.refs_0_), channel_id=1, source_target_pairs={{0,16},{2,18},{4,20},{6,22},{8,24},{10,26},{12,28},{14,30},{16,0},... | collective-permute-start | bytes 786440 | tf_op jit(solution)/shard_map/ppermute | solution.py:487
  47.0 21.7 %collective-permute-start.9 = (bf16[64,2048]{1,0:T(8,128)(2,1)}, bf16[64,2048]{1,0:T(8,128)(2,1)}, u32[]{:S(2)}, u32[]{:S(2)}) collective-permute-start(bf16[64,2048]{1,0:T(8,128)(2,1)} %get-tuple-element.123.refs_0_), channel_id=1, source_target_pairs={{0,24},{2,26},{4,28},{6,30},{8,16},{10,18},{12,20},{14,22},{16,8},... | collective-permute-start | bytes 786440 | tf_op jit(solution)/shard_map/ppermute | solution.py:487
  72.3 204.8 %reduce-scatter.2.cloned.1.call-start = ((), (), s32[]{:S(2)}) async-start(), calls=%async_computation.2 | async-start | bytes 8912896 | tf_op jit(solution)/shard_map/reduce_scatter | solution.py:729
  72.4 7.7 %collective-permute-start.10 = (bf16[4,64,2048]{2,1,0:T(8,128)(2,1)S(1)}, bf16[4,64,2048]{2,1,0:T(8,128)(2,1)}, u32[]{:S(2)}, u32[]{:S(2)}) collective-permute-start(bf16[4,64,2048]{2,1,0:T(8,128)(2,1)S(1)} %copy-done.1), channel_id=1, source_target_pairs={{0,2},{2,0},{4,6},{6,4},{8,10},{10,8},{12,14},{14,12},{16,18},{18,... | collective-permute-start | bytes 3145736 | tf_op jit(solution)/shard_map/ppermute | solution.py:487
  72.4 7.6 %collective-permute-start.11 = (bf16[4,64,2048]{2,1,0:T(8,128)(2,1)}, bf16[4,64,2048]{2,1,0:T(8,128)(2,1)}, u32[]{:S(2)}, u32[]{:S(2)}) collective-permute-start(bf16[4,64,2048]{2,1,0:T(8,128)(2,1)} %get-tuple-element.128.refs_7_), channel_id=1, source_target_pairs={{0,2},{2,0},{4,6},{6,4},{8,10},{10,8},{12,14},{14,12},{16,18},{18,... | collective-permute-start | bytes 3145736 | tf_op jit(solution)/shard_map/ppermute | solution.py:487
  74.1 28.5 %collective-permute-start.13 = (bf16[4,64,2048]{2,1,0:T(8,128)(2,1)}, bf16[4,64,2048]{2,1,0:T(8,128)(2,1)S(1)}, u32[]{:S(2)}, u32[]{:S(2)}) collective-permute-start(bf16[4,64,2048]{2,1,0:T(8,128)(2,1)} %get-tuple-element.129.refs_9_.refs_6_), channel_id=1, source_target_pairs={{0,4},{2,6},{4,0},{6,2},{8,12},{10,14},{12,8},{14,10},{16,20},{18,... | collective-permute-start | bytes 3145736 | tf_op jit(solution)/shard_map/ppermute | solution.py:487
  74.7 28.9 %collective-permute-start.12 = (bf16[4,64,2048]{2,1,0:T(8,128)(2,1)}, bf16[4,64,2048]{2,1,0:T(8,128)(2,1)S(1)}, u32[]{:S(2)}, u32[]{:S(2)}) collective-permute-start(bf16[4,64,2048]{2,1,0:T(8,128)(2,1)} %get-tuple-element.129.refs_9_.refs_6_), channel_id=1, source_target_pairs={{0,2},{2,0},{4,6},{6,4},{8,10},{10,8},{12,14},{14,12},{16,18},{18,... | collective-permute-start | bytes 3145736 | tf_op jit(solution)/shard_map/ppermute | solution.py:487
  103.6 2.9 %collective-permute-start.14 = (bf16[4,64,2048]{2,1,0:T(8,128)(2,1)}, bf16[4,64,2048]{2,1,0:T(8,128)(2,1)S(1)}, u32[]{:S(2)}, u32[]{:S(2)}) collective-permute-start(bf16[4,64,2048]{2,1,0:T(8,128)(2,1)} %hold.12.refs_8_), channel_id=1, source_target_pairs={{0,2},{2,0},{4,6},{6,4},{8,10},{10,8},{12,14},{14,12},{16,18},{18,... | collective-permute-start | bytes 3145736 | tf_op jit(solution)/shard_map/ppermute | solution.py:487
  159.2 2.9 %collective-permute-start.15 = (bf16[8,64,1024]{2,1,0:T(8,128)(2,1)}, bf16[8,64,1024]{2,1,0:T(8,128)(2,1)S(1)}, u32[]{:S(2)}, u32[]{:S(2)}) collective-permute-start(bf16[8,64,1024]{2,1,0:T(8,128)(2,1)} %get-tuple-element.140), channel_id=1, source_target_pairs={{0,2},{2,0},{4,6},{6,4},{8,10},{10,8},{12,14},{14,12},{16,18},{18,... | collective-permute-start | bytes 3145736 | tf_op jit(solution)/shard_map/ppermute | solution.py:487
  159.4 33.6 %collective-permute-start.17 = (bf16[512,1024]{1,0:T(8,128)(2,1)}, bf16[512,1024]{1,0:T(8,128)(2,1)S(1)}, u32[]{:S(2)}, u32[]{:S(2)}) collective-permute-start(bf16[512,1024]{1,0:T(8,128)(2,1)} %get-tuple-element.143), channel_id=1, source_target_pairs={{0,1},{1,0},{2,3},{3,2},{4,5},{5,4},{6,7},{7,6},{8,9},{9,8},{10,11... | collective-permute-start | bytes 3145736 | tf_op jit(solution)/shard_map/ppermute | solution.py:491
  165.6 27.5 %collective-permute-start.16 = (bf16[4,64,1024]{2,1,0:T(8,128)(2,1)}, bf16[4,64,1024]{2,1,0:T(8,128)(2,1)S(1)}, u32[]{:S(2)}, u32[]{:S(2)}) collective-permute-start(bf16[4,64,1024]{2,1,0:T(8,128)(2,1)} %get-tuple-element.141.refs_14_), channel_id=1, source_target_pairs={{0,4},{2,6},{4,0},{6,2},{8,12},{10,14},{12,8},{14,10},{16,20},{18,... | collective-permute-start | bytes 1572872 | tf_op jit(solution)/shard_map/ppermute | solution.py:487
  194.2 3.0 %collective-permute-start.18 = (bf16[8,64,1024]{2,1,0:T(8,128)(2,1)}, bf16[8,64,1024]{2,1,0:T(8,128)(2,1)S(1)}, u32[]{:S(2)}, u32[]{:S(2)}) collective-permute-start(bf16[8,64,1024]{2,1,0:T(8,128)(2,1)} %get-tuple-element.150), channel_id=1, source_target_pairs={{0,2},{2,0},{4,6},{6,4},{8,10},{10,8},{12,14},{14,12},{16,18},{18,... | collective-permute-start | bytes 3145736 | tf_op jit(solution)/shard_map/ppermute | solution.py:487
  195.7 1.5 collective-permute-start.19
  200.8 15.4 %collective-permute-start.20 = (bf16[4,64,1024]{2,1,0:T(8,128)(2,1)}, bf16[4,64,1024]{2,1,0:T(8,128)(2,1)S(1)}, u32[]{:S(2)}, u32[]{:S(2)}) collective-permute-start(bf16[4,64,1024]{2,1,0:T(8,128)(2,1)} %get-tuple-element.160.refs_2_), channel_id=1, source_target_pairs={{0,4},{2,6},{4,0},{6,2},{8,12},{10,14},{12,8},{14,10},{16,20},{18,... | collective-permute-start | bytes 1572872 | tf_op jit(solution)/shard_map/ppermute | solution.py:487
  202.1 10.0 %collective-permute-start.21 = (bf16[128,1024]{1,0:T(8,128)(2,1)}, bf16[128,1024]{1,0:T(8,128)(2,1)S(1)}, u32[]{:S(2)}, u32[]{:S(2)}) collective-permute-start(bf16[128,1024]{1,0:T(8,128)(2,1)} %get-tuple-element.163), channel_id=1, source_target_pairs={{0,1},{1,0},{2,3},{3,2},{4,5},{5,4},{6,7},{7,6},{8,9},{9,8},{10,11... | collective-permute-start | bytes 786440 | tf_op jit(solution)/shard_map/ppermute | solution.py:491
  202.6 13.6 %collective-permute-start.22 = (bf16[512,256]{1,0:T(8,128)(2,1)}, bf16[512,256]{1,0:T(8,128)(2,1)S(1)}, u32[]{:S(2)}, u32[]{:S(2)}) collective-permute-start(bf16[512,256]{1,0:T(8,128)(2,1)} %get-tuple-element.164), channel_id=1, source_target_pairs={{0,1},{1,0},{2,3},{3,2},{4,5},{5,4},{6,7},{7,6},{8,9},{9,8},{10,11... | collective-permute-start | bytes 786440 | tf_op jit(solution)/shard_map/ppermute | solution.py:491
  204.2 4.0 %collective-permute-start.23 = (f32[1,8704]{1,0:T(1,128)S(1)}, f32[1,8704]{1,0:T(1,128)S(1)}, u32[]{:S(2)}, u32[]{:S(2)}) collective-permute-start(f32[1,8704]{1,0:T(1,128)S(1)} %add.26), channel_id=1, source_target_pairs={{0,8},{2,10},{4,12},{6,14},{8,0},{10,2},{12,4},{14,6},{16,24},{18,... | collective-permute-start | bytes 104456 | tf_op jit(solution)/shard_map/ppermute | solution.py:487
  204.2 5.5 %collective-permute-start.24 = (f32[1,8704]{1,0:T(1,128)S(1)}, f32[1,8704]{1,0:T(1,128)S(1)}, u32[]{:S(2)}, u32[]{:S(2)}) collective-permute-start(f32[1,8704]{1,0:T(1,128)S(1)} %add.26), channel_id=1, source_target_pairs={{0,16},{2,18},{4,20},{6,22},{8,24},{10,26},{12,28},{14,30},{16,0},... | collective-permute-start | bytes 104456 | tf_op jit(solution)/shard_map/ppermute | solution.py:487
  208.2 8.0 %copy-start.24 = (f32[1,8704]{1,0:T(1,128)}, f32[1,8704]{1,0:T(1,128)S(1)}, u32[]{:S(2)}) copy-start(f32[1,8704]{1,0:T(1,128)S(1)} %collective-permute-done.23.refs_3_) | copy-start | bytes 104452
  208.2 3.9 %collective-permute-start.25 = (f32[1,8704]{1,0:T(1,128)S(1)}, f32[1,8704]{1,0:T(1,128)S(1)}, u32[]{:S(2)}, u32[]{:S(2)}) collective-permute-start(f32[1,8704]{1,0:T(1,128)S(1)} %add.26), channel_id=1, source_target_pairs={{0,24},{2,26},{4,28},{6,30},{8,16},{10,18},{12,20},{14,22},{16,8},... | collective-permute-start | bytes 104456 | tf_op jit(solution)/shard_map/ppermute | solution.py:487
  209.7 6.5 %copy-start.26 = (f32[1,8704]{1,0:T(1,128)}, f32[1,8704]{1,0:T(1,128)S(1)}, u32[]{:S(2)}) copy-start(f32[1,8704]{1,0:T(1,128)S(1)} %collective-permute-done.24.refs_4_) | copy-start | bytes 104452
  217.7 11.5 %copy-start.36 = (f32[1024]{0:T(1024)S(1)}, f32[1024]{0:T(1024)}, u32[]{:S(2)}) copy-start(f32[1024]{0:T(1024)} %param.35) | copy-start | bytes 12292
  217.7 11.4 %copy-start.37 = (f32[1024]{0:T(1024)S(1)}, f32[1024]{0:T(1024)}, u32[]{:S(2)}) copy-start(f32[1024]{0:T(1024)} %param.31) | copy-start | bytes 12292
  222.4 41.6 %collective-permute-start.26 = (bf16[384,1024]{1,0:T(8,128)(2,1)}, bf16[384,1024]{1,0:T(8,128)(2,1)S(1)}, u32[]{:S(2)}, u32[]{:S(2)}) collective-permute-start(bf16[384,1024]{1,0:T(8,128)(2,1)} %get-tuple-element.181), channel_id=1, source_target_pairs={{0,1},{1,0},{2,3},{3,2},{4,5},{5,4},{6,7},{7,6},{8,9},{9,8},{10,11... | collective-permute-start | bytes 2359304 | tf_op jit(solution)/shard_map/ppermute | solution.py:491
  223.4 23.3 %collective-permute-start.28 = (bf16[1,64,2048]{2,1,0:T(8,128)(2,1)}, bf16[1,64,2048]{2,1,0:T(8,128)(2,1)S(1)}, u32[]{:S(2)}, u32[]{:S(2)}) collective-permute-start(bf16[1,64,2048]{2,1,0:T(8,128)(2,1)} %get-tuple-element.178.refs_3_), channel_id=1, source_target_pairs={{0,8},{2,10},{4,12},{6,14},{8,0},{10,2},{12,4},{14,6},{16,24},{18,... | collective-permute-start | bytes 786440 | tf_op jit(solution)/shard_map/ppermute | solution.py:487
  223.8 27.3 %collective-permute-start.29 = (bf16[1,64,2048]{2,1,0:T(8,128)(2,1)}, bf16[1,64,2048]{2,1,0:T(8,128)(2,1)S(1)}, u32[]{:S(2)}, u32[]{:S(2)}) collective-permute-start(bf16[1,64,2048]{2,1,0:T(8,128)(2,1)} %get-tuple-element.179.refs_4_), channel_id=1, source_target_pairs={{0,16},{2,18},{4,20},{6,22},{8,24},{10,26},{12,28},{14,30},{16,0},... | collective-permute-start | bytes 786440 | tf_op jit(solution)/shard_map/ppermute | solution.py:487
  226.9 37.1 %collective-permute-start.30 = (bf16[1,64,2048]{2,1,0:T(8,128)(2,1)}, bf16[1,64,2048]{2,1,0:T(8,128)(2,1)S(1)}, u32[]{:S(2)}, u32[]{:S(2)}) collective-permute-start(bf16[1,64,2048]{2,1,0:T(8,128)(2,1)} %get-tuple-element.180.refs_5_), channel_id=1, source_target_pairs={{0,24},{2,26},{4,28},{6,30},{8,16},{10,18},{12,20},{14,22},{16,8},... | collective-permute-start | bytes 786440 | tf_op jit(solution)/shard_map/ppermute | solution.py:487
  226.9 6.5 %collective-permute-start.27 = (f32[1,8704]{1,0:T(1,128)}, f32[1,8704]{1,0:T(1,128)S(1)}, u32[]{:S(2)}, u32[]{:S(2)}) collective-permute-start(f32[1,8704]{1,0:T(1,128)} %get-tuple-element.182), channel_id=1, source_target_pairs={{0,4},{2,6},{4,0},{6,2},{8,12},{10,14},{12,8},{14,10},{16,20},{18,... | collective-permute-start | bytes 104456 | tf_op jit(solution)/shard_map/ppermute | solution.py:487
  233.4 32.2 %copy-start.16 = (f32[1,8704]{1,0:T(1,128)S(1)}, f32[1,8704]{1,0:T(1,128)}, u32[]{:S(2)}) copy-start(f32[1,8704]{1,0:T(1,128)} %get-tuple-element.182) | copy-start | bytes 104452
  233.4 30.6 %copy-start.21 = (f32[1,8704]{1,0:T(1,128)}, f32[1,8704]{1,0:T(1,128)S(1)}, u32[]{:S(2)}) copy-start(f32[1,8704]{1,0:T(1,128)S(1)} %collective-permute-done.27.refs_1_) | copy-start | bytes 104452
  246.7 17.3 %copy-start.11 = (bf16[1,64,2048]{2,1,0:T(8,128)(2,1)}, bf16[1,64,2048]{2,1,0:T(8,128)(2,1)S(1)}, u32[]{:S(2)}) copy-start(bf16[1,64,2048]{2,1,0:T(8,128)(2,1)S(1)} %collective-permute-done.28.refs_3_) | copy-start | bytes 786436
  251.1 12.9 %copy-start.13 = (bf16[1,64,2048]{2,1,0:T(8,128)(2,1)}, bf16[1,64,2048]{2,1,0:T(8,128)(2,1)S(1)}, u32[]{:S(2)}) copy-start(bf16[1,64,2048]{2,1,0:T(8,128)(2,1)S(1)} %collective-permute-done.29.refs_4_) | copy-start | bytes 786436
  266.4 8.9 %collective-permute-start.31 = (f32[1,8704]{1,0:T(1,128)S(1)}, f32[1,8704]{1,0:T(1,128)S(1)}, u32[]{:S(2)}, u32[]{:S(2)}) collective-permute-start(f32[1,8704]{1,0:T(1,128)S(1)} %get-tuple-element.194), channel_id=1, source_target_pairs={{0,1},{1,0},{2,3},{3,2},{4,5},{5,4},{6,7},{7,6},{8,9},{9,8},{10,11... | collective-permute-start | bytes 104456 | tf_op jit(solution)/shard_map/ppermute | solution.py:491
  (32 other events, 68.5 us)
Sparse Core Ops, SparseCore 0:
  72.4 54.2 all-gather.1
  130.8 128.7 reduce-scatter.1
where the time goes:
time: 291 us; the launch traced here: 287 us
  Pallas kernels  140 us (48%)
  waiting for transfers between devices  77.3 us (27%)
  starting transfers between devices  30.6 us (11%)
  local copies, waits for them, and re-layouts  19.2 us (7%)
  between operations  14.6 us (5%)
  other arithmetic  4.69 us (2%)
    ppermute x24, waiting for transfers between devices, swap_dp(): return lax.ppermute(array, 'dp', [(i, i ^ bits) for i in range(count)])  57.9 us
    pallas_call x2, Pallas kernels, attention_call(): pl.pallas_call(kernel, grid_spec=pltpu.PrefetchScalarGridSpec(num_scalar_...  53.7 us
    pallas_call x2, Pallas kernels, mlp_call(): pl.pallas_call(kernel, grid_spec=pltpu.PrefetchScalarGridSpec(num_scalar_...  44.4 us
    ppermute x24, starting transfers between devices, swap_dp(): return lax.ppermute(array, 'dp', [(i, i ^ bits) for i in range(count)])  22.7 us
    ppermute x8, waiting for transfers between devices, swap_tensor(): return lax.ppermute(array, 'tensor', [(0, 1), (1, 0)])  19.3 us
    unnamed x94, local copies, waits for them, and re-layouts  15.3 us
    pallas_call x2, Pallas kernels, two_sided(): pl.pallas_call(kernel, grid_spec=pltpu.PrefetchScalarGridSpec(num_scalar_...  12.6 us
    pallas_call x3, Pallas kernels, add_split(): pl.pallas_call(kernel, grid=(len(pairs) * steps,), in_specs=[part(index)...  8.95 us
  transfers between devices with their start and end apart: 34, of which 14 were waited for; matrix products, arithmetic and copies ran while one was open for 4% of the time, Pallas kernels for 47%

commit v1 on v0

--- a/solution.py
+++ b/solution.py
@@ -794,13 +794,11 @@
         output = finish_output(
             inputs, [branch_home, branch_other], biases, ctx_other, attn_wide.reshape(width, -1), columns + pairs * PAIR
         )
-        share_second, small_other, *sent = hold(
-            [swap_tensor(share_second), swap_dp(small, 2), *sent], output
-        )
+        grad_inputs = finish_input(inputs, cotangent, share_home, [share_first, swap_tensor(share_second)])
+        small_other, *sent = hold([swap_dp(small, 2), *sent], output, grad_inputs)
         small = small + small_other
         small = small + swap_tensor(jnp.where(jnp.arange(small.shape[1]) < columns + units, 0.0, small))
-        grad_inputs = finish_input(inputs, cotangent, share_home, [share_first, share_second])
-        (mlp_sum,) = hold([mlp_sum], grad_inputs)
+        (mlp_sum,) = hold([mlp_sum], sent[0])
         grad_up, grad_down_t = finish_weights([[mlp_sum]], block, block)
         attn_sources = [sent]
         small = small[0]

time: 291 us -> 285 us (0.979)
  waiting for transfers between devices: 77.3 us -> 71.5 us
    ppermute x24, waiting for transfers between devices: 57.9 us -> 43.9 us  [swap_dp(): return lax.ppermute(array, 'dp', [(i, i ^ bits) for i in range(count)])]
    ppermute x8, waiting for transfers between devices: 19.3 us -> 27.6 us  [swap_tensor(): return lax.ppermute(array, 'tensor', [(0, 1), (1, 0)])]
  transfers between devices with their start and end apart: 34 -> 34, of which waited for: 14 -> 15; matrix products, arithmetic and copies ran while one was open for 4% -> 4% of each run, Pallas kernels for 47% -> 48%
where the time goes in v1:
time: 285 us; the launch traced here: 281 us
  Pallas kernels  140 us (49%)
  waiting for transfers between devices  71.5 us (25%)
  starting transfers between devices  30.6 us (11%)
  local copies, waits for them, and re-layouts  19.3 us (7%)
  between operations  14.6 us (5%)
  other arithmetic  4.69 us (2%)
    pallas_call x2, Pallas kernels, attention_call(): pl.pallas_call(kernel, grid_spec=pltpu.PrefetchScalarGridSpec(num_scalar_...  53.7 us
    pallas_call x2, Pallas kernels, mlp_call(): pl.pallas_call(kernel, grid_spec=pltpu.PrefetchScalarGridSpec(num_scalar_...  44.4 us
    ppermute x24, waiting for transfers between devices, swap_dp(): return lax.ppermute(array, 'dp', [(i, i ^ bits) for i in range(count)])  43.9 us
    ppermute x8, waiting for transfers between devices, swap_tensor(): return lax.ppermute(array, 'tensor', [(0, 1), (1, 0)])  27.6 us
    ppermute x24, starting transfers between devices, swap_dp(): return lax.ppermute(array, 'dp', [(i, i ^ bits) for i in range(count)])  22.7 us
    unnamed x94, local copies, waits for them, and re-layouts  15.4 us
    pallas_call x2, Pallas kernels, two_sided(): pl.pallas_call(kernel, grid_spec=pltpu.PrefetchScalarGridSpec(num_scalar_...  12.6 us
    pallas_call x3, Pallas kernels, add_split(): pl.pallas_call(kernel, grid=(len(pairs) * steps,), in_specs=[part(index)...  8.95 us
  transfers between devices with their start and end apart: 34, of which 15 were waited for; matrix products, arithmetic and copies ran while one was open for 4% of the time, Pallas kernels for 48%

profile of v1, /device:TPU:8, one launch (start us, length us, event | category | flops | bytes accessed | tf_op | source)
XLA Modules:
  0.0 281.1 jit_solution(5861248644419009182)
XLA Ops:
  7.2 1.6 collective-permute-start
  8.8 2.0 interleave.1
  11.2 2.6 collective-permute-start.2
  15.5 2.3 copy.67.refs_0_
  17.9 15.3 %collective-permute-done.4.refs_5_ = bf16[64,256]{1,0:T(8,128)(2,1)S(1)} collective-permute-done((bf16[64,256]{1,0:T(8,128)(2,1)S(1)}, bf16[64,256]{1,0:T(8,128)(2,1)S(1)}, u32[]{:S(2)}, u32[]{:S(2)}) %collective-permute-start.4) | collective-permute-done | bytes 32800 | tf_op jit(solution)/shard_map/ppermute | solution.py:491
  33.1 3.7 %collective-permute-done.3.refs_3_ = bf16[64,2048]{1,0:T(8,128)(2,1)S(1)} collective-permute-done((bf16[64,2048]{1,0:T(8,128)(2,1)}, bf16[64,2048]{1,0:T(8,128)(2,1)S(1)}, u32[]{:S(2)}, u32[]{:S(2)}) %collective-permute-start.3) | collective-permute-done | bytes 262176 | tf_op jit(solution)/shard_map/ppermute | solution.py:487
  37.6 1.0 copy-done
  38.5 2.1 join.2.refs_2_.refs_5_
  41.9 1.5 collective-permute-start.6
  44.0 3.0 %collective-permute-start.8 = (bf16[64,2048]{1,0:T(8,128)(2,1)}, bf16[64,2048]{1,0:T(8,128)(2,1)}, u32[]{:S(2)}, u32[]{:S(2)}) collective-permute-start(bf16[64,2048]{1,0:T(8,128)(2,1)} %get-tuple-element.122.refs_0_), channel_id=1, source_target_pairs={{0,16},{2,18},{4,20},{6,22},{8,24},{10,26},{12,28},{14,30},{16,0},... | collective-permute-start | bytes 786440 | tf_op jit(solution)/shard_map/ppermute | solution.py:487
  48.2 7.3 %norm_kernel.1 = (bf16[1024,1024]{1,0:T(8,128)(2,1)}, bf16[1024,1024]{1,0:T(8,128)(2,1)}, bf16[1024,1024]{1,0:T(8,128)(2,1)}, bf16[1024,1024]{1,0:T(8,128)(2,1)}, bf16[1024,1024]{1,0:T(8,128)(2,1)}) custom-call(s32[1]{0:T(128)} %bitcast.3.place, bf16[512,1024]{1,0:T(8,128)(2,1)} %x.5, bf16[512,1024]{1,0:T(8,128)(2,1)} %copy-done, ...), custom_call_target="tpu_custom_call" | custom-call | tf_op jit(solution)/shard_map/norm_kernel/pallas_call | solution.py:143
  55.5 9.0 %collective-permute-done.8.refs_2_ = bf16[64,2048]{1,0:T(8,128)(2,1)} collective-permute-done((bf16[64,2048]{1,0:T(8,128)(2,1)}, bf16[64,2048]{1,0:T(8,128)(2,1)}, u32[]{:S(2)}, u32[]{:S(2)}) %collective-permute-start.8) | collective-permute-done | bytes 262176 | tf_op jit(solution)/shard_map/ppermute | solution.py:487
  64.5 4.2 %collective-permute-done.9.refs_3_ = bf16[64,2048]{1,0:T(8,128)(2,1)} collective-permute-done((bf16[64,2048]{1,0:T(8,128)(2,1)}, bf16[64,2048]{1,0:T(8,128)(2,1)}, u32[]{:S(2)}, u32[]{:S(2)}) %collective-permute-start.9) | collective-permute-done | bytes 262176 | tf_op jit(solution)/shard_map/ppermute | solution.py:487
  68.8 2.2 join.3.refs_1_
  70.9 0.9 copy-done.4
  74.7 5.4 %turn_kernel.1 = (bf16[1024,1024]{1,0:T(8,128)(2,1)}, bf16[1024,1024]{1,0:T(8,128)(2,1)}, f32[1,1024]{1,0:T(1,128)}) custom-call(s32[1]{0:T(128)} %bitcast.3.place, bf16[512,1024]{1,0:T(8,128)(2,1)} %dy.1, bf16[512,1024]{1,0:T(8,128)(2,1)} %copy-done.4), custom_call_target="tpu_custom_call" | custom-call | tf_op jit(solution)/shard_map/turn_kernel/pallas_call | solution.py:143
  80.1 21.6 %mlp_both_ways.2 = (bf16[16,64,4096]{2,1,0:T(8,128)(2,1)}, f32[1,1024]{1,0:T(1,128)}, f32[1024,1024]{1,0:T(8,128)}, f32[1024,1024]{1,0:T(8,128)}) custom-call(s32[2,16]{1,0:T(2,128)} %pad_add_fusion.1.order, bf16[1024,1024]{1,0:T(8,128)(2,1)} %get-tuple-element.125.refs_0_.refs_1_, bf16[1024,1024]{1,0:T(8,128)(2,1)} %get-tuple-element.119.refs_1_.refs_2_, ...), custom_call_target="tpu_custom_call" | custom-call | flops 12884901888 | bytes 33554432 | tf_op jit(solution)/shard_map/mlp_both_ways/pallas_call | solution.py:274
  101.7 1.0 collective-permute-done.13.refs_0_
  102.6 1.0 copy-done.7
  103.6 2.9 %collective-permute-done.14.refs_9_ = bf16[4,64,2048]{2,1,0:T(8,128)(2,1)S(1)} collective-permute-done((bf16[4,64,2048]{2,1,0:T(8,128)(2,1)}, bf16[4,64,2048]{2,1,0:T(8,128)(2,1)S(1)}, u32[]{:S(2)}, u32[]{:S(2)}) %collective-permute-start.14) | collective-permute-done | bytes 1048608 | tf_op jit(solution)/shard_map/ppermute | solution.py:487
  106.5 1.0 copy-done.43
  107.5 22.8 %mlp_both_ways.3 = (bf16[16,64,4096]{2,1,0:T(8,128)(2,1)}, f32[1,1024]{1,0:T(1,128)}, f32[1024,1024]{1,0:T(8,128)}, f32[1024,1024]{1,0:T(8,128)}, f32[2,1024]{1,0:T(2,128)}) custom-call(s32[2,16]{1,0:T(2,128)} %pad_add_fusion.1.order, bf16[16,64,4096]{2,1,0:T(8,128)(2,1)} %get-tuple-element.129.refs_0_, ...), custom_call_target="tpu_custom_call", output_to_operand_aliasing={{0}: (1, {})} | custom-call | flops 12884901888 | bytes 33554432 | tf_op jit(solution)/shard_map/mlp_both_ways/pallas_call | solution.py:274
  132.2 27.0 %attention_both_ways.2 = (bf16[8,64,1024]{2,1,0:T(8,128)(2,1)}, bf16[8,64,1024]{2,1,0:T(8,128)(2,1)}, f32[1,768]{1,0:T(1,128)}, f32[1024,1024]{1,0:T(8,128)}, f3...) custom-call(s32[3,16]{1,0:T(4,128)} %pad_add_fusion.order, bf16[1024,1024]{1,0:T(8,128)(2,1)} %get-tuple-element.115.refs_3_.refs_0_, ...), custom_call_target="tpu_custom_call" | custom-call | flops 21474836480 | bytes 33554432 | tf_op jit(solution)/shard_map/attention_both_ways/pallas_call | solution.py:470
  160.1 2.1 collective-permute-done.15.refs_1_
  162.2 1.0 copy-done.8
  163.2 2.4 add_split.3
  166.3 26.8 %attention_both_ways.3 = (bf16[8,64,1024]{2,1,0:T(8,128)(2,1)}, bf16[8,64,1024]{2,1,0:T(8,128)(2,1)}, f32[1,768]{1,0:T(1,128)}, f32[2,1024]{1,0:T(2,128)}, f32[5...) custom-call(s32[3,16]{1,0:T(4,128)} %pad_add_fusion.order, ...), custom_call_target="tpu_custom_call" | custom-call | flops 21474836480 | bytes 33554432 | tf_op jit(solution)/shard_map/attention_both_ways/pallas_call | solution.py:470
  194.3 1.4 flatten_rows.1
  196.2 1.1 collective-permute-done.19.refs_2_
  198.3 2.5 add_split.4
  200.8 1.3 collective-permute-start.20
  202.6 1.5 collective-permute-start.22
  204.2 3.0 %collective-permute-start.24 = (f32[1,8704]{1,0:T(1,128)S(1)}, f32[1,8704]{1,0:T(1,128)S(1)}, u32[]{:S(2)}, u32[]{:S(2)}) collective-permute-start(f32[1,8704]{1,0:T(1,128)S(1)} %add.26), channel_id=1, source_target_pairs={{0,16},{2,18},{4,20},{6,22},{8,24},{10,26},{12,28},{14,30},{16,0},... | collective-permute-start | bytes 104456 | tf_op jit(solution)/shard_map/ppermute | solution.py:487
  208.2 1.5 collective-permute-start.25
  209.7 2.4 collective-permute-done.25.refs_5_
  212.1 4.1 %collective-permute-done.22.refs_2_ = bf16[512,256]{1,0:T(8,128)(2,1)S(1)} collective-permute-done((bf16[512,256]{1,0:T(8,128)(2,1)}, bf16[512,256]{1,0:T(8,128)(2,1)S(1)}, u32[]{:S(2)}, u32[]{:S(2)}) %collective-permute-start.22) | collective-permute-done | bytes 262176 | tf_op jit(solution)/shard_map/ppermute | solution.py:491
  217.7 4.0 %add_split.5 = (bf16[1,64,2048]{2,1,0:T(8,128)(2,1)}, bf16[1,64,2048]{2,1,0:T(8,128)(2,1)}, bf16[1,64,2048]{2,1,0:T(8,128)(2,1)}, bf16[1,64,2048]{2,1,0:T(8,128)(2,1)}) custom-call(bf16[4,64,1024]{2,1,0:T(8,128)(2,1)} %get-tuple-element.172.refs_0_, bf16[4,64,1024]{2,1,0:T(8,128)(2,1)} %get-tuple-element.173.refs_1_, ...), custom_call_target="tpu_custom_call" | custom-call | tf_op jit(solution)/shard_map/add_split/pallas_call | solution.py:685
  222.4 1.0 collective-permute-start.26
  223.8 3.1 %collective-permute-start.29 = (bf16[1,64,2048]{2,1,0:T(8,128)(2,1)}, bf16[1,64,2048]{2,1,0:T(8,128)(2,1)S(1)}, u32[]{:S(2)}, u32[]{:S(2)}) collective-permute-start(bf16[1,64,2048]{2,1,0:T(8,128)(2,1)} %get-tuple-element.178.refs_4_), channel_id=1, source_target_pairs={{0,16},{2,18},{4,20},{6,22},{8,24},{10,26},{12,28},{14,30},{16,0},... | collective-permute-start | bytes 786440 | tf_op jit(solution)/shard_map/ppermute | solution.py:487
  226.9 2.2 collective-permute-start.27
  229.8 3.6 %finish_output.1.refs_5_ = bf16[512,1024]{1,0:T(8,128)(2,1)} custom-call(bf16[512,1024]{1,0:T(8,128)(2,1)} %x.5, f32[2,1024]{1,0:T(2,128)} %pad_maximum_fusion.2.bias, f32[512,1024]{1,0:T(8,128)} %get-tuple-element.141.refs_0_, bf16[512,1024]{1,0:T(8,128)(2,1)} %get-tuple-element.148.refs_1_, bf16[512,256]{1,0:T(8,128)(2,1)} %get-tuple-element.165.refs_2_, ...), custom_call_target="tpu_custom_call" | custom-call | tf_op jit(solution)/shard_map/finish_output/pallas_call | solution.py:608
  233.4 7.9 %collective-permute-done.26.refs_1_ = bf16[384,1024]{1,0:T(8,128)(2,1)S(1)} collective-permute-done((bf16[384,1024]{1,0:T(8,128)(2,1)}, bf16[384,1024]{1,0:T(8,128)(2,1)S(1)}, u32[]{:S(2)}, u32[]{:S(2)}) %collective-permute-start.26) | collective-permute-done | bytes 786464 | tf_op jit(solution)/shard_map/ppermute | solution.py:491
  242.2 5.3 %finish_input.1.refs_6_ = f32[512,1024]{1,0:T(8,128)} custom-call(bf16[512,1024]{1,0:T(8,128)(2,1)} %x.5, bf16[512,1024]{1,0:T(8,128)(2,1)} %dy.1, f32[512,1024]{1,0:T(8,128)} %get-tuple-element.166.home, bf16[128,1024]{1,0:T(8,128)(2,1)} %get-tuple-element.167.refs_0_, bf16[384,1024]{1,0:T(8,128)(2,1)} %copy-done.15), custom_call_target="tpu_custom_call" | custom-call | tf_op jit(solution)/shard_map/finish_input/pallas_call | solution.py:640
  247.5 3.6 %collective-permute-done.29.refs_3_ = bf16[1,64,2048]{2,1,0:T(8,128)(2,1)S(1)} collective-permute-done((bf16[1,64,2048]{2,1,0:T(8,128)(2,1)}, bf16[1,64,2048]{2,1,0:T(8,128)(2,1)S(1)}, u32[]{:S(2)}, u32[]{:S(2)}) %collective-permute-start.29) | collective-permute-done | bytes 262176 | tf_op jit(solution)/shard_map/ppermute | solution.py:487
  251.1 12.9 %collective-permute-done.30.refs_4_ = bf16[1,64,2048]{2,1,0:T(8,128)(2,1)S(1)} collective-permute-done((bf16[1,64,2048]{2,1,0:T(8,128)(2,1)}, bf16[1,64,2048]{2,1,0:T(8,128)(2,1)S(1)}, u32[]{:S(2)}, u32[]{:S(2)}) %collective-permute-start.30) | collective-permute-done | bytes 262176 | tf_op jit(solution)/shard_map/ppermute | solution.py:487
  265.5 1.5 collective-permute-start.31
  267.1 2.1 finish_weights.2
  271.4 2.1 finish_weights.3
  (164 shorter events, 25.0 us)
Async XLA Ops:
  7.2 125.1 %all-gather.2.cloned.1.call-start = ((), (), s32[]{:S(2)}) async-start(), calls=%async_computation.1 | async-start | bytes 5013504 | tf_op jit(solution)/shard_map/all_gather | solution.py:726
  7.2 29.6 %collective-permute-start = (bf16[512,1024]{1,0:T(8,128)(2,1)}, bf16[512,1024]{1,0:T(8,128)(2,1)S(1)}, u32[]{:S(2)}, u32[]{:S(2)}) collective-permute-start(bf16[512,1024]{1,0:T(8,128)(2,1)} %x.5), channel_id=1, source_target_pairs={{0,1},{1,0},{2,3},{3,2},{4,5},{5,4},{6,7},{7,6},{8,9},{9,8},{10,11... | collective-permute-start | bytes 3145736 | tf_op jit(solution)/shard_map/ppermute | solution.py:491
  10.8 22.3 %collective-permute-start.1 = (bf16[64,2048]{1,0:T(8,128)(2,1)}, bf16[64,2048]{1,0:T(8,128)(2,1)S(1)}, u32[]{:S(2)}, u32[]{:S(2)}) collective-permute-start(bf16[64,2048]{1,0:T(8,128)(2,1)} %get-tuple-element.117.refs_0_), channel_id=1, source_target_pairs={{0,8},{2,10},{4,12},{6,14},{8,0},{10,2},{12,4},{14,6},{16,24},{18,... | collective-permute-start | bytes 786440 | tf_op jit(solution)/shard_map/ppermute | solution.py:487
  11.2 21.9 %collective-permute-start.2 = (bf16[64,2048]{1,0:T(8,128)(2,1)}, bf16[64,2048]{1,0:T(8,128)(2,1)S(1)}, u32[]{:S(2)}, u32[]{:S(2)}) collective-permute-start(bf16[64,2048]{1,0:T(8,128)(2,1)} %get-tuple-element.117.refs_0_), channel_id=1, source_target_pairs={{0,16},{2,18},{4,20},{6,22},{8,24},{10,26},{12,28},{14,30},{16,0},... | collective-permute-start | bytes 786440 | tf_op jit(solution)/shard_map/ppermute | solution.py:487
  13.8 23.0 %collective-permute-start.3 = (bf16[64,2048]{1,0:T(8,128)(2,1)}, bf16[64,2048]{1,0:T(8,128)(2,1)S(1)}, u32[]{:S(2)}, u32[]{:S(2)}) collective-permute-start(bf16[64,2048]{1,0:T(8,128)(2,1)} %get-tuple-element.117.refs_0_), channel_id=1, source_target_pairs={{0,24},{2,26},{4,28},{6,30},{8,16},{10,18},{12,20},{14,22},{16,8},... | collective-permute-start | bytes 786440 | tf_op jit(solution)/shard_map/ppermute | solution.py:487
  15.0 18.1 %collective-permute-start.4 = (bf16[64,256]{1,0:T(8,128)(2,1)S(1)}, bf16[64,256]{1,0:T(8,128)(2,1)S(1)}, u32[]{:S(2)}, u32[]{:S(2)}) collective-permute-start(bf16[64,256]{1,0:T(8,128)(2,1)S(1)} %slice.80), channel_id=1, source_target_pairs={{0,1},{1,0},{2,3},{3,2},{4,5},{5,4},{6,7},{7,6},{8,9},{9,8},{10,11... | collective-permute-start | bytes 98312 | tf_op jit(solution)/shard_map/ppermute | solution.py:491
  17.8 25.6 %copy-start.38 = (f32[1024]{0:T(1024)S(1)}, f32[1024]{0:T(1024)}, u32[]{:S(2)}) copy-start(f32[1024]{0:T(1024)} %param.27) | copy-start | bytes 12292
  17.8 25.6 %copy-start.39 = (f32[1024]{0:T(1024)S(1)}, f32[1024]{0:T(1024)}, u32[]{:S(2)}) copy-start(f32[1024]{0:T(1024)} %param.25) | copy-start | bytes 12292
  17.8 25.6 %copy-start.40 = (f32[1024]{0:T(1024)S(1)}, f32[1024]{0:T(1024)}, u32[]{:S(2)}) copy-start(f32[1024]{0:T(1024)} %param.26) | copy-start | bytes 12292
  17.8 25.6 %copy-start.41 = (f32[1024]{0:T(1024)S(1)}, f32[1024]{0:T(1024)}, u32[]{:S(2)}) copy-start(f32[1024]{0:T(1024)} %param.24) | copy-start | bytes 12292
  17.8 29.7 %copy-start.20 = (bf16[64,2048]{1,0:T(8,128)(2,1)S(1)}, bf16[64,2048]{1,0:T(8,128)(2,1)}, u32[]{:S(2)}) copy-start(bf16[64,2048]{1,0:T(8,128)(2,1)} %get-tuple-element.123) | copy-start | bytes 786436
  40.7 6.8 %copy-start.32 = (bf16[64,256]{1,0:T(8,128)(2,1)S(1)}, bf16[64,256]{1,0:T(8,128)(2,1)}, u32[]{:S(2)}) copy-start(bf16[64,256]{1,0:T(8,128)(2,1)} %copy-done.31) | copy-start | bytes 98308
  40.7 30.2 %collective-permute-start.5 = (bf16[512,1024]{1,0:T(8,128)(2,1)}, bf16[512,1024]{1,0:T(8,128)(2,1)S(1)}, u32[]{:S(2)}, u32[]{:S(2)}) collective-permute-start(bf16[512,1024]{1,0:T(8,128)(2,1)} %get-tuple-element.118), channel_id=1, source_target_pairs={{0,1},{1,0},{2,3},{3,2},{4,5},{5,4},{6,7},{7,6},{8,9},{9,8},{10,11... | collective-permute-start | bytes 3145736 | tf_op jit(solution)/shard_map/ppermute | solution.py:491
  41.9 29.0 %collective-permute-start.6 = (bf16[4,64,2048]{2,1,0:T(8,128)(2,1)S(1)}, bf16[4,64,2048]{2,1,0:T(8,128)(2,1)S(1)}, u32[]{:S(2)}, u32[]{:S(2)}) collective-permute-start(bf16[4,64,2048]{2,1,0:T(8,128)(2,1)S(1)} %copy-done.1), channel_id=1, source_target_pairs={{0,4},{2,6},{4,0},{6,2},{8,12},{10,14},{12,8},{14,10},{16,20},{18,... | collective-permute-start | bytes 3145736 | tf_op jit(solution)/shard_map/ppermute | solution.py:487
  44.0 11.5 %collective-permute-start.7 = (bf16[64,2048]{1,0:T(8,128)(2,1)}, bf16[64,2048]{1,0:T(8,128)(2,1)}, u32[]{:S(2)}, u32[]{:S(2)}) collective-permute-start(bf16[64,2048]{1,0:T(8,128)(2,1)} %get-tuple-element.122.refs_0_), channel_id=1, source_target_pairs={{0,8},{2,10},{4,12},{6,14},{8,0},{10,2},{12,4},{14,6},{16,24},{18,... | collective-permute-start | bytes 786440 | tf_op jit(solution)/shard_map/ppermute | solution.py:487
  44.0 20.5 %collective-permute-start.8 = (bf16[64,2048]{1,0:T(8,128)(2,1)}, bf16[64,2048]{1,0:T(8,128)(2,1)}, u32[]{:S(2)}, u32[]{:S(2)}) collective-permute-start(bf16[64,2048]{1,0:T(8,128)(2,1)} %get-tuple-element.122.refs_0_), channel_id=1, source_target_pairs={{0,16},{2,18},{4,20},{6,22},{8,24},{10,26},{12,28},{14,30},{16,0},... | collective-permute-start | bytes 786440 | tf_op jit(solution)/shard_map/ppermute | solution.py:487
  47.0 21.7 %collective-permute-start.9 = (bf16[64,2048]{1,0:T(8,128)(2,1)}, bf16[64,2048]{1,0:T(8,128)(2,1)}, u32[]{:S(2)}, u32[]{:S(2)}) collective-permute-start(bf16[64,2048]{1,0:T(8,128)(2,1)} %get-tuple-element.122.refs_0_), channel_id=1, source_target_pairs={{0,24},{2,26},{4,28},{6,30},{8,16},{10,18},{12,20},{14,22},{16,8},... | collective-permute-start | bytes 786440 | tf_op jit(solution)/shard_map/ppermute | solution.py:487
  72.3 199.1 %reduce-scatter.2.cloned.1.call-start = ((), (), s32[]{:S(2)}) async-start(), calls=%async_computation.2 | async-start | bytes 8912896 | tf_op jit(solution)/shard_map/reduce_scatter | solution.py:729
  72.4 7.7 %collective-permute-start.10 = (bf16[4,64,2048]{2,1,0:T(8,128)(2,1)S(1)}, bf16[4,64,2048]{2,1,0:T(8,128)(2,1)}, u32[]{:S(2)}, u32[]{:S(2)}) collective-permute-start(bf16[4,64,2048]{2,1,0:T(8,128)(2,1)S(1)} %copy-done.1), channel_id=1, source_target_pairs={{0,2},{2,0},{4,6},{6,4},{8,10},{10,8},{12,14},{14,12},{16,18},{18,... | collective-permute-start | bytes 3145736 | tf_op jit(solution)/shard_map/ppermute | solution.py:487
  72.4 7.6 %collective-permute-start.11 = (bf16[4,64,2048]{2,1,0:T(8,128)(2,1)}, bf16[4,64,2048]{2,1,0:T(8,128)(2,1)}, u32[]{:S(2)}, u32[]{:S(2)}) collective-permute-start(bf16[4,64,2048]{2,1,0:T(8,128)(2,1)} %get-tuple-element.127.refs_7_), channel_id=1, source_target_pairs={{0,2},{2,0},{4,6},{6,4},{8,10},{10,8},{12,14},{14,12},{16,18},{18,... | collective-permute-start | bytes 3145736 | tf_op jit(solution)/shard_map/ppermute | solution.py:487
  74.1 28.5 %collective-permute-start.13 = (bf16[4,64,2048]{2,1,0:T(8,128)(2,1)}, bf16[4,64,2048]{2,1,0:T(8,128)(2,1)S(1)}, u32[]{:S(2)}, u32[]{:S(2)}) collective-permute-start(bf16[4,64,2048]{2,1,0:T(8,128)(2,1)} %get-tuple-element.128.refs_9_.refs_6_), channel_id=1, source_target_pairs={{0,4},{2,6},{4,0},{6,2},{8,12},{10,14},{12,8},{14,10},{16,20},{18,... | collective-permute-start | bytes 3145736 | tf_op jit(solution)/shard_map/ppermute | solution.py:487
  74.7 28.9 %collective-permute-start.12 = (bf16[4,64,2048]{2,1,0:T(8,128)(2,1)}, bf16[4,64,2048]{2,1,0:T(8,128)(2,1)S(1)}, u32[]{:S(2)}, u32[]{:S(2)}) collective-permute-start(bf16[4,64,2048]{2,1,0:T(8,128)(2,1)} %get-tuple-element.128.refs_9_.refs_6_), channel_id=1, source_target_pairs={{0,2},{2,0},{4,6},{6,4},{8,10},{10,8},{12,14},{14,12},{16,18},{18,... | collective-permute-start | bytes 3145736 | tf_op jit(solution)/shard_map/ppermute | solution.py:487
  103.6 2.9 %collective-permute-start.14 = (bf16[4,64,2048]{2,1,0:T(8,128)(2,1)}, bf16[4,64,2048]{2,1,0:T(8,128)(2,1)S(1)}, u32[]{:S(2)}, u32[]{:S(2)}) collective-permute-start(bf16[4,64,2048]{2,1,0:T(8,128)(2,1)} %hold.12.refs_8_), channel_id=1, source_target_pairs={{0,2},{2,0},{4,6},{6,4},{8,10},{10,8},{12,14},{14,12},{16,18},{18,... | collective-permute-start | bytes 3145736 | tf_op jit(solution)/shard_map/ppermute | solution.py:487
  159.2 2.9 %collective-permute-start.15 = (bf16[8,64,1024]{2,1,0:T(8,128)(2,1)}, bf16[8,64,1024]{2,1,0:T(8,128)(2,1)S(1)}, u32[]{:S(2)}, u32[]{:S(2)}) collective-permute-start(bf16[8,64,1024]{2,1,0:T(8,128)(2,1)} %get-tuple-element.139), channel_id=1, source_target_pairs={{0,2},{2,0},{4,6},{6,4},{8,10},{10,8},{12,14},{14,12},{16,18},{18,... | collective-permute-start | bytes 3145736 | tf_op jit(solution)/shard_map/ppermute | solution.py:487
  159.4 33.6 %collective-permute-start.17 = (bf16[512,1024]{1,0:T(8,128)(2,1)}, bf16[512,1024]{1,0:T(8,128)(2,1)S(1)}, u32[]{:S(2)}, u32[]{:S(2)}) collective-permute-start(bf16[512,1024]{1,0:T(8,128)(2,1)} %get-tuple-element.142), channel_id=1, source_target_pairs={{0,1},{1,0},{2,3},{3,2},{4,5},{5,4},{6,7},{7,6},{8,9},{9,8},{10,11... | collective-permute-start | bytes 3145736 | tf_op jit(solution)/shard_map/ppermute | solution.py:491
  165.6 27.5 %collective-permute-start.16 = (bf16[4,64,1024]{2,1,0:T(8,128)(2,1)}, bf16[4,64,1024]{2,1,0:T(8,128)(2,1)S(1)}, u32[]{:S(2)}, u32[]{:S(2)}) collective-permute-start(bf16[4,64,1024]{2,1,0:T(8,128)(2,1)} %get-tuple-element.140.refs_14_), channel_id=1, source_target_pairs={{0,4},{2,6},{4,0},{6,2},{8,12},{10,14},{12,8},{14,10},{16,20},{18,... | collective-permute-start | bytes 1572872 | tf_op jit(solution)/shard_map/ppermute | solution.py:487
  194.2 3.0 %collective-permute-start.18 = (bf16[8,64,1024]{2,1,0:T(8,128)(2,1)}, bf16[8,64,1024]{2,1,0:T(8,128)(2,1)S(1)}, u32[]{:S(2)}, u32[]{:S(2)}) collective-permute-start(bf16[8,64,1024]{2,1,0:T(8,128)(2,1)} %get-tuple-element.149), channel_id=1, source_target_pairs={{0,2},{2,0},{4,6},{6,4},{8,10},{10,8},{12,14},{14,12},{16,18},{18,... | collective-permute-start | bytes 3145736 | tf_op jit(solution)/shard_map/ppermute | solution.py:487
  195.7 1.5 collective-permute-start.19
  200.8 15.4 %collective-permute-start.20 = (bf16[4,64,1024]{2,1,0:T(8,128)(2,1)}, bf16[4,64,1024]{2,1,0:T(8,128)(2,1)S(1)}, u32[]{:S(2)}, u32[]{:S(2)}) collective-permute-start(bf16[4,64,1024]{2,1,0:T(8,128)(2,1)} %get-tuple-element.159.refs_2_), channel_id=1, source_target_pairs={{0,4},{2,6},{4,0},{6,2},{8,12},{10,14},{12,8},{14,10},{16,20},{18,... | collective-permute-start | bytes 1572872 | tf_op jit(solution)/shard_map/ppermute | solution.py:487
  202.1 10.0 %collective-permute-start.21 = (bf16[128,1024]{1,0:T(8,128)(2,1)}, bf16[128,1024]{1,0:T(8,128)(2,1)S(1)}, u32[]{:S(2)}, u32[]{:S(2)}) collective-permute-start(bf16[128,1024]{1,0:T(8,128)(2,1)} %get-tuple-element.162), channel_id=1, source_target_pairs={{0,1},{1,0},{2,3},{3,2},{4,5},{5,4},{6,7},{7,6},{8,9},{9,8},{10,11... | collective-permute-start | bytes 786440 | tf_op jit(solution)/shard_map/ppermute | solution.py:491
  202.6 13.6 %collective-permute-start.22 = (bf16[512,256]{1,0:T(8,128)(2,1)}, bf16[512,256]{1,0:T(8,128)(2,1)S(1)}, u32[]{:S(2)}, u32[]{:S(2)}) collective-permute-start(bf16[512,256]{1,0:T(8,128)(2,1)} %get-tuple-element.163), channel_id=1, source_target_pairs={{0,1},{1,0},{2,3},{3,2},{4,5},{5,4},{6,7},{7,6},{8,9},{9,8},{10,11... | collective-permute-start | bytes 786440 | tf_op jit(solution)/shard_map/ppermute | solution.py:491
  204.2 4.0 %collective-permute-start.23 = (f32[1,8704]{1,0:T(1,128)S(1)}, f32[1,8704]{1,0:T(1,128)S(1)}, u32[]{:S(2)}, u32[]{:S(2)}) collective-permute-start(f32[1,8704]{1,0:T(1,128)S(1)} %add.26), channel_id=1, source_target_pairs={{0,8},{2,10},{4,12},{6,14},{8,0},{10,2},{12,4},{14,6},{16,24},{18,... | collective-permute-start | bytes 104456 | tf_op jit(solution)/shard_map/ppermute | solution.py:487
  204.2 5.5 %collective-permute-start.24 = (f32[1,8704]{1,0:T(1,128)S(1)}, f32[1,8704]{1,0:T(1,128)S(1)}, u32[]{:S(2)}, u32[]{:S(2)}) collective-permute-start(f32[1,8704]{1,0:T(1,128)S(1)} %add.26), channel_id=1, source_target_pairs={{0,16},{2,18},{4,20},{6,22},{8,24},{10,26},{12,28},{14,30},{16,0},... | collective-permute-start | bytes 104456 | tf_op jit(solution)/shard_map/ppermute | solution.py:487
  208.2 8.0 %copy-start.23 = (f32[1,8704]{1,0:T(1,128)}, f32[1,8704]{1,0:T(1,128)S(1)}, u32[]{:S(2)}) copy-start(f32[1,8704]{1,0:T(1,128)S(1)} %collective-permute-done.23.refs_3_) | copy-start | bytes 104452
  208.2 3.9 %collective-permute-start.25 = (f32[1,8704]{1,0:T(1,128)S(1)}, f32[1,8704]{1,0:T(1,128)S(1)}, u32[]{:S(2)}, u32[]{:S(2)}) collective-permute-start(f32[1,8704]{1,0:T(1,128)S(1)} %add.26), channel_id=1, source_target_pairs={{0,24},{2,26},{4,28},{6,30},{8,16},{10,18},{12,20},{14,22},{16,8},... | collective-permute-start | bytes 104456 | tf_op jit(solution)/shard_map/ppermute | solution.py:487
  209.7 6.5 %copy-start.25 = (f32[1,8704]{1,0:T(1,128)}, f32[1,8704]{1,0:T(1,128)S(1)}, u32[]{:S(2)}) copy-start(f32[1,8704]{1,0:T(1,128)S(1)} %collective-permute-done.24.refs_4_) | copy-start | bytes 104452
  217.7 11.5 %copy-start.36 = (f32[1024]{0:T(1024)S(1)}, f32[1024]{0:T(1024)}, u32[]{:S(2)}) copy-start(f32[1024]{0:T(1024)} %param.35) | copy-start | bytes 12292
  217.7 11.4 %copy-start.37 = (f32[1024]{0:T(1024)S(1)}, f32[1024]{0:T(1024)}, u32[]{:S(2)}) copy-start(f32[1024]{0:T(1024)} %param.31) | copy-start | bytes 12292
  222.4 18.9 %collective-permute-start.26 = (bf16[384,1024]{1,0:T(8,128)(2,1)}, bf16[384,1024]{1,0:T(8,128)(2,1)S(1)}, u32[]{:S(2)}, u32[]{:S(2)}) collective-permute-start(bf16[384,1024]{1,0:T(8,128)(2,1)} %get-tuple-element.180), channel_id=1, source_target_pairs={{0,1},{1,0},{2,3},{3,2},{4,5},{5,4},{6,7},{7,6},{8,9},{9,8},{10,11... | collective-permute-start | bytes 2359304 | tf_op jit(solution)/shard_map/ppermute | solution.py:491
  223.4 24.1 %collective-permute-start.28 = (bf16[1,64,2048]{2,1,0:T(8,128)(2,1)}, bf16[1,64,2048]{2,1,0:T(8,128)(2,1)S(1)}, u32[]{:S(2)}, u32[]{:S(2)}) collective-permute-start(bf16[1,64,2048]{2,1,0:T(8,128)(2,1)} %get-tuple-element.177.refs_3_), channel_id=1, source_target_pairs={{0,8},{2,10},{4,12},{6,14},{8,0},{10,2},{12,4},{14,6},{16,24},{18,... | collective-permute-start | bytes 786440 | tf_op jit(solution)/shard_map/ppermute | solution.py:487
  223.8 27.3 %collective-permute-start.29 = (bf16[1,64,2048]{2,1,0:T(8,128)(2,1)}, bf16[1,64,2048]{2,1,0:T(8,128)(2,1)S(1)}, u32[]{:S(2)}, u32[]{:S(2)}) collective-permute-start(bf16[1,64,2048]{2,1,0:T(8,128)(2,1)} %get-tuple-element.178.refs_4_), channel_id=1, source_target_pairs={{0,16},{2,18},{4,20},{6,22},{8,24},{10,26},{12,28},{14,30},{16,0},... | collective-permute-start | bytes 786440 | tf_op jit(solution)/shard_map/ppermute | solution.py:487
  226.9 37.1 %collective-permute-start.30 = (bf16[1,64,2048]{2,1,0:T(8,128)(2,1)}, bf16[1,64,2048]{2,1,0:T(8,128)(2,1)S(1)}, u32[]{:S(2)}, u32[]{:S(2)}) collective-permute-start(bf16[1,64,2048]{2,1,0:T(8,128)(2,1)} %get-tuple-element.179.refs_5_), channel_id=1, source_target_pairs={{0,24},{2,26},{4,28},{6,30},{8,16},{10,18},{12,20},{14,22},{16,8},... | collective-permute-start | bytes 786440 | tf_op jit(solution)/shard_map/ppermute | solution.py:487
  226.9 20.5 %collective-permute-start.27 = (f32[1,8704]{1,0:T(1,128)}, f32[1,8704]{1,0:T(1,128)S(1)}, u32[]{:S(2)}, u32[]{:S(2)}) collective-permute-start(f32[1,8704]{1,0:T(1,128)} %get-tuple-element.181), channel_id=1, source_target_pairs={{0,4},{2,6},{4,0},{6,2},{8,12},{10,14},{12,8},{14,10},{16,20},{18,... | collective-permute-start | bytes 104456 | tf_op jit(solution)/shard_map/ppermute | solution.py:487
  247.4 17.3 %copy-start.16 = (f32[1,8704]{1,0:T(1,128)S(1)}, f32[1,8704]{1,0:T(1,128)}, u32[]{:S(2)}) copy-start(f32[1,8704]{1,0:T(1,128)} %get-tuple-element.181) | copy-start | bytes 104452
  247.5 16.6 %copy-start.30 = (f32[1,8704]{1,0:T(1,128)}, f32[1,8704]{1,0:T(1,128)S(1)}, u32[]{:S(2)}) copy-start(f32[1,8704]{1,0:T(1,128)S(1)} %collective-permute-done.27.refs_0_) | copy-start | bytes 104452
  247.5 16.5 %copy-start.12 = (bf16[1,64,2048]{2,1,0:T(8,128)(2,1)}, bf16[1,64,2048]{2,1,0:T(8,128)(2,1)S(1)}, u32[]{:S(2)}) copy-start(bf16[1,64,2048]{2,1,0:T(8,128)(2,1)S(1)} %collective-permute-done.28.refs_2_) | copy-start | bytes 786436
  251.1 12.9 %copy-start.13 = (bf16[1,64,2048]{2,1,0:T(8,128)(2,1)}, bf16[1,64,2048]{2,1,0:T(8,128)(2,1)S(1)}, u32[]{:S(2)}) copy-start(bf16[1,64,2048]{2,1,0:T(8,128)(2,1)S(1)} %collective-permute-done.29.refs_3_) | copy-start | bytes 786436
  265.5 4.0 %collective-permute-start.31 = (f32[1,8704]{1,0:T(1,128)S(1)}, f32[1,8704]{1,0:T(1,128)S(1)}, u32[]{:S(2)}, u32[]{:S(2)}) collective-permute-start(f32[1,8704]{1,0:T(1,128)S(1)} %get-tuple-element.192), channel_id=1, source_target_pairs={{0,1},{1,0},{2,3},{3,2},{4,5},{5,4},{6,7},{7,6},{8,9},{9,8},{10,11... | collective-permute-start | bytes 104456 | tf_op jit(solution)/shard_map/ppermute | solution.py:491
  (32 other events, 68.5 us)
Sparse Core Ops, SparseCore 0:
  72.4 54.2 all-gather.1
  130.8 128.7 reduce-scatter.1
